TPU v7x, 32 devices: a whole 2x2x4 slice. The times are simulated.
32 devices in a mesh: section: 2 (over x), seq: 4 (over y, core), tensor: 4 (over z).
Axes of the slice: x: 2, y: 2, z: 4, core: 2. Of those that a mesh axis runs over, the one named last changes fastest.
Arguments:
- tokens: bfloat16 [2, 2048, 1024], P(None, ('seq', 'tensor')), may hold values from -6 to 6
- w_qkv: bfloat16 [2, 1024, 3, 1024], P('section', None, None, 'tensor'), may hold values from -0.1875 to 0.1875
- w_out: bfloat16 [2, 1024, 1024], P('section', 'tensor'), may hold values from -0.25 to 0.25
- w_gate_up: bfloat16 [2, 1024, 2, 2816], P('section', None, None, 'tensor'), may hold values from -0.1875 to 0.1875
- w_down: bfloat16 [2, 2816, 1024], P('section', 'tensor'), may hold values from -0.109375 to 0.109375
- norm_gains: float32 [2, 2, 1024], P('section'), may hold values from 0.5 to 1.5
- log_decay: float32 [2, 2048, 16], P(None, 'seq', 'tensor'), may hold values from -2 to 0
- segment_ids: int32 [2, 2048], P(None, 'seq'), may hold values from 0 to 4, as said below
- cotangent: bfloat16 [2, 2048, 1024], P(None, ('seq', 'tensor')), may hold values from -6 to 6
Outputs:
- layer_outputs: bfloat16 [2, 2, 2048, 1024], P('section', None, ('seq', 'tensor'))
- input_grads: float32 [2, 2, 2048, 1024], P('section', None, ('seq', 'tensor'))
- grad_qkv: float32 [2, 1024, 3, 1024], P('section', None, None, 'tensor')
- grad_out: float32 [2, 1024, 1024], P('section', 'tensor')
- grad_gate_up: float32 [2, 1024, 2, 2816], P('section', None, None, 'tensor')
- grad_down: float32 [2, 2816, 1024], P('section', 'tensor')
- grad_gains: float32 [2, 2, 1024], P('section')
Inputs may be any that keep to these rules, and one draw needn't show every extreme that they name: `segment_ids`: within a stream the ids never fall and number the documents from 0. One stream, drawn from the seed, holds five documents, and the one with id 2 starts within the first 512 tokens and ends within the last 512. In the other, a document ends near every multiple of 2048 tokens before the stream's end, within 512 of it on either side.
All inputs are finite; a program needn't handle non-finite values.
Results may differ from a plain program's by a relative error of at most 0.03.
Values may be sent and summed in bfloat16 or wider, within the bound.
No kernel may reach another device: no remote copies, remote signals or barrier semaphores. Data moves between devices by JAX's collectives and lax.ppermute only.
A program may use at most 192 MiB of HBM per device.

v0:
```python
import jax
import jax.numpy as jnp
from jax import lax
from jax.sharding import PartitionSpec as P

HDIM = 64
BLOCK = 64


epsilon = 1e-05
head_epsilon = 1.0
highest = lax.Precision.HIGHEST
far_below = -1e30
sentinel = 1000000000.0


def carried_in(array, axis, combine, identity, reverse):
    count, here = (lax.axis_size(axis), lax.axis_index(axis))
    everything = jax.tree.map(
        lambda part, kind: lax.all_gather(part.astype(kind), axis),
        array,
        jax.tree.map(lambda a: jnp.bfloat16 if a.dtype == jnp.float32 else a.dtype, array),
    )
    start = jax.tree.map(
        lambda part, zero: jnp.broadcast_to(jnp.asarray(zero, part.dtype), part.shape),
        array,
        identity,
    )

    def lap(k, before):
        at = count - 1 - k if reverse else k
        reached = at > here if reverse else at < here
        new = combine(
            before, jax.tree.map(lambda part, own: part[at].astype(own.dtype), everything, array)
        )
        return jax.tree.map(lambda a, b: jnp.where(reached, a, b), new, before)

    return lax.fori_loop(0, count, lap, start)


def from_behind(value, axis, steps):
    count = lax.axis_size(axis)
    initial, last = (max(0, -steps), min(count, count - steps))
    return lax.ppermute(value, axis, [(source, source + steps) for source in range(initial, last)])


def rms_scale(values):
    return lax.rsqrt(jnp.mean(values * values, axis=-1, keepdims=True) + epsilon)


def head_scale(values):
    return lax.rsqrt(jnp.mean(values * values, axis=-1, keepdims=True) + head_epsilon)


def rms_back(values, row_scale, gain_row, grad_normed):
    unit_rows = values * row_scale
    grad_unit = grad_normed * gain_row
    grad_values = row_scale * (
        grad_unit - unit_rows * jnp.mean(grad_unit * unit_rows, axis=-1, keepdims=True)
    )
    return (grad_values, jnp.sum(grad_normed * unit_rows, axis=0))


def gather_rows(shard_piece):
    return lax.all_gather(shard_piece, "tensor", axis=0, tiled=True)


def scatter_rows(partial_sum):
    return lax.psum_scatter(
        partial_sum.astype(jnp.bfloat16), "tensor", scatter_dimension=0, tiled=True
    ).astype(jnp.float32)


def gather_grads(shard_piece):
    return lax.all_gather(shard_piece, "tensor", axis=0, tiled=True)


def scatter_grads(partial_sum):
    return lax.psum_scatter(
        partial_sum.astype(jnp.bfloat16), "tensor", scatter_dimension=0, tiled=True
    ).astype(jnp.float32)


def place_at(stacked, member, position, active):
    previous = lax.dynamic_index_in_dim(stacked, position, 0, keepdims=False)
    return lax.dynamic_update_index_in_dim(
        stacked, jnp.where(active, member, previous), position, 0
    )


def join_forward(earlier, later):
    first_early, last_early, decay_early, state_early = earlier
    first_late, last_late, decay_late, state_late = later
    linked = jnp.where(
        (last_early == first_late) | (last_early < 0.0) | (first_late > 0.5 * sentinel), 1.0, 0.0
    )
    carried = decay_late * linked
    return (
        jnp.minimum(first_early, first_late),
        jnp.maximum(last_early, last_late),
        decay_early * carried,
        carried[..., None, None] * state_early + state_late,
    )


def join_backward(earlier, later):
    decay_early, grad_early = earlier
    decay_late, grad_late = later
    return (decay_late * decay_early, grad_late + decay_late[..., None, None] * grad_early)


def chain_forward(summary):
    heads_local = summary[2].shape[0]
    identity = (
        jnp.array(sentinel, jnp.float32),
        jnp.array(-1.0, jnp.float32),
        jnp.ones((heads_local,), jnp.float32),
        jnp.zeros((heads_local, HDIM, HDIM), jnp.float32),
    )
    return carried_in(summary, "seq", join_forward, identity, False)


def chain_backward(summary):
    identity = (jnp.ones_like(summary[0]), jnp.zeros_like(summary[1]))
    return carried_in(summary, "seq", join_backward, identity, True)


def block_mask(segment_blocks):
    span = segment_blocks.shape[1]
    causal = jnp.arange(span)[:, None] >= jnp.arange(span)[None, :]
    return causal[None] & (segment_blocks[:, :, None] == segment_blocks[:, None, :])


def diag_scores(query_blocks, key_blocks, allowed):
    dots = jnp.einsum(
        "bqhd,bkhd->bhqk", query_blocks, key_blocks, preferred_element_type=jnp.float32
    )
    return jnp.where(allowed[:, None], dots * HDIM ** (-0.5), far_below)


def diag_forward(query_blocks, key_blocks, value_blocks, allowed):
    scores = diag_scores(query_blocks, key_blocks, allowed)
    highest_score = jnp.max(scores, axis=-1, keepdims=True)
    powers = jnp.exp(scores - highest_score)
    totals = jnp.sum(powers, axis=-1, keepdims=True)
    weights = (powers / totals).astype(jnp.bfloat16)
    attended = jnp.einsum(
        "bhqk,bkhd->bqhd", weights, value_blocks, preferred_element_type=jnp.float32
    )
    return (attended, highest_score + jnp.log(totals))


def diag_backward(query_blocks, key_blocks, value_blocks, allowed, logsum, grad_attended):
    probs = jnp.exp(diag_scores(query_blocks, key_blocks, allowed) - logsum)
    grad_probs = jnp.einsum(
        "bqhd,bkhd->bhqk", grad_attended, value_blocks, preferred_element_type=jnp.float32
    )
    grad_values = jnp.einsum(
        "bhqk,bqhd->bkhd",
        probs.astype(jnp.bfloat16),
        grad_attended,
        preferred_element_type=jnp.float32,
    )
    centre = jnp.sum(grad_probs * probs, axis=-1, keepdims=True)
    grad_scores = (probs * (grad_probs - centre)).astype(jnp.bfloat16)
    grad_query = jnp.einsum(
        "bhqk,bkhd->bqhd", grad_scores, key_blocks, preferred_element_type=jnp.float32
    ) * HDIM ** (-0.5)
    grad_keys = jnp.einsum(
        "bhqk,bqhd->bkhd", grad_scores, query_blocks, preferred_element_type=jnp.float32
    ) * HDIM ** (-0.5)
    return (grad_query, grad_keys, grad_values)


def norm_local(key_blocks, value_blocks, decay_blocks, segment_blocks):
    cumul = jnp.cumsum(decay_blocks, axis=1)
    totals = cumul[:, -1]
    starts = segment_blocks[:, 0]
    finals = segment_blocks[:, -1]
    kept = jnp.exp(totals[:, None] - cumul) * (segment_blocks == finals[:, None])[:, :, None]
    weighted = key_blocks.astype(jnp.float32) * kept[..., None]
    block_states = jnp.einsum(
        "bkhd,bkhe->bhde", weighted, value_blocks.astype(jnp.float32), precision=highest
    )
    block_decay = jnp.exp(totals) * (starts == finals)[:, None]
    before = jnp.concatenate([starts[:1], finals[:-1]])
    internal_connections = block_decay * (before == starts)[:, None]

    def advance(state, element):
        return (element[0][:, None, None] * state + element[1], state)

    device_state, exclusive = lax.scan(
        advance,
        jnp.zeros(block_states.shape[1:], jnp.float32),
        (internal_connections, block_states),
    )
    device_decay = jnp.exp(jnp.sum(totals, axis=0)) * (starts[0] == finals[-1])
    summary = (starts[0], finals[-1], device_decay, device_state)
    return (cumul, kept, block_decay, before, exclusive, summary)


def norm_incoming(cumul, segment_blocks, block_decay, before, exclusive, prefix):
    before = jnp.concatenate([prefix[1][None], before[1:]])
    links = block_decay * (before == segment_blocks[:, 0])[:, None]
    through = jnp.cumprod(links, axis=0)
    through = jnp.concatenate([jnp.ones_like(links[:1]), through[:-1]])
    incoming = exclusive + through[..., None, None] * prefix[3]
    reach = jnp.exp(cumul) * (segment_blocks == before[:, None])[:, :, None]
    return (links, incoming, reach)


def decay_weight(cumul, allowed):
    spread = jnp.transpose(cumul[:, :, None, :] - cumul[:, None, :, :], (0, 3, 1, 2))
    masked = allowed[:, None]
    return jnp.where(masked, jnp.exp(jnp.where(masked, spread, 0.0)), 0.0)


def norm_values(query_blocks, key_blocks, value_blocks, weight, incoming, reach):
    dots = jnp.einsum(
        "bqhd,bkhd->bhqk", query_blocks, key_blocks, preferred_element_type=jnp.float32
    )
    scored = (dots * weight).astype(jnp.bfloat16)
    inner = jnp.einsum("bhqk,bkhd->bqhd", scored, value_blocks, preferred_element_type=jnp.float32)
    outer = reach[..., None] * jnp.einsum(
        "bqhd,bhde->bqhe", query_blocks.astype(jnp.float32), incoming, precision=highest
    )
    return (inner + outer, scored)


def norm_backward(
    query_blocks,
    key_blocks,
    value_blocks,
    decay_blocks,
    segment_blocks,
    allowed,
    prefix,
    grad_normed,
):
    cumul, kept, block_decay, before, exclusive, summary = norm_local(
        key_blocks, value_blocks, decay_blocks, segment_blocks
    )
    links, incoming, reach = norm_incoming(
        cumul, segment_blocks, block_decay, before, exclusive, prefix
    )
    weight = decay_weight(cumul, allowed)
    norm_raw, scored = norm_values(query_blocks, key_blocks, value_blocks, weight, incoming, reach)
    out_scale = head_scale(norm_raw)
    unit_out = norm_raw * out_scale
    grad_raw = (
        out_scale
        * (grad_normed - unit_out * jnp.mean(grad_normed * unit_out, axis=-1, keepdims=True))
    ).astype(jnp.bfloat16)
    grad_scored = jnp.einsum(
        "bqhe,bkhe->bhqk", grad_raw, value_blocks, preferred_element_type=jnp.float32
    )
    grad_values = jnp.einsum(
        "bhqk,bqhe->bkhe", scored, grad_raw, preferred_element_type=jnp.float32
    )
    grad_dots = (grad_scored * weight).astype(jnp.bfloat16)
    grad_wide = grad_raw.astype(jnp.float32)
    grad_query = jnp.einsum(
        "bhqk,bkhd->bqhd", grad_dots, key_blocks, preferred_element_type=jnp.float32
    )
    grad_query = grad_query + reach[..., None] * jnp.einsum(
        "bqhe,bhde->bqhd", grad_wide, incoming, precision=highest
    )
    grad_keys = jnp.einsum(
        "bhqk,bqhd->bkhd", grad_dots, query_blocks, preferred_element_type=jnp.float32
    )
    grad_incoming = jnp.einsum(
        "bqhd,bqhe->bhde",
        query_blocks.astype(jnp.float32) * reach[..., None],
        grad_wide,
        precision=highest,
    )

    def retreat(carry, element):
        pending, through = carry
        return (
            (element[1] + element[0][:, None, None] * pending, element[0] * through),
            (pending, through),
        )

    start = (jnp.zeros_like(grad_incoming[0]), jnp.ones_like(links[0]))
    own_total, stacked = lax.scan(retreat, start, (links, grad_incoming), reverse=True)
    later_grad = chain_backward((own_total[1], own_total[0]))[1]
    ends_grad = stacked[0] + stacked[1][..., None, None] * later_grad
    grad_keys = grad_keys + kept[..., None] * jnp.einsum(
        "bkhe,bhde->bkhd", value_blocks.astype(jnp.float32), ends_grad, precision=highest
    )
    grad_values = grad_values + jnp.einsum(
        "bkhd,bhde->bkhe",
        key_blocks.astype(jnp.float32) * kept[..., None],
        ends_grad,
        precision=highest,
    )
    return (grad_query, grad_keys, grad_values)


def split_blocks(chosen, decays, segments):
    length = chosen.shape[0]
    count = length // BLOCK
    heads_local = chosen.shape[2]
    query_blocks = chosen[:, 0].reshape(count, BLOCK, heads_local, HDIM)
    key_blocks = chosen[:, 1].reshape(count, BLOCK, heads_local, HDIM)
    value_blocks = chosen[:, 2].reshape(count, BLOCK, heads_local, HDIM)
    segment_blocks = segments.reshape(count, BLOCK)
    decay_blocks = decays.reshape(count, BLOCK, heads_local)
    return (query_blocks, key_blocks, value_blocks, decay_blocks, segment_blocks)


def layer_forward(token_rows, weights, decays, segments, section_first):
    w_qkv, w_out, w_gate_up, w_down, gain_pair = weights
    normed_full = gather_rows(
        (token_rows * rms_scale(token_rows) * gain_pair[0]).astype(jnp.bfloat16)
    )
    length = normed_full.shape[0]
    heads_local = w_qkv.shape[-1] // HDIM
    projected = jnp.einsum("td,dcf->tcf", normed_full, w_qkv, preferred_element_type=jnp.float32)
    projected = projected.reshape(length, 3, heads_local, HDIM)
    sigmoid = jax.nn.sigmoid(projected[:, :2])
    slopes = sigmoid * (1.0 + projected[:, :2] * (1.0 - sigmoid))
    softened = jnp.concatenate([projected[:, :2] * sigmoid, projected[:, 2:]], axis=1)
    chosen = jnp.where(section_first, projected, softened).astype(jnp.bfloat16)
    query_blocks, key_blocks, value_blocks, decay_blocks, segment_blocks = split_blocks(
        chosen, decays, segments
    )
    allowed = block_mask(segment_blocks)
    diag_out, logsum = diag_forward(query_blocks, key_blocks, value_blocks, allowed)
    cumul, kept, block_decay, before, exclusive, summary = norm_local(
        key_blocks, value_blocks, decay_blocks, segment_blocks
    )
    prefix = chain_forward(summary)
    links, incoming, reach = norm_incoming(
        cumul, segment_blocks, block_decay, before, exclusive, prefix
    )
    norm_raw = norm_values(
        query_blocks, key_blocks, value_blocks, decay_weight(cumul, allowed), incoming, reach
    )[0]
    norm_out = norm_raw * head_scale(norm_raw)
    mixed = (
        jnp.where(section_first, diag_out, norm_out)
        .astype(jnp.bfloat16)
        .reshape(length, heads_local * HDIM)
    )
    middle = token_rows + scatter_rows(jnp.dot(mixed, w_out, preferred_element_type=jnp.float32))
    hidden_in = gather_rows((middle * rms_scale(middle) * gain_pair[1]).astype(jnp.bfloat16))
    gate_up = jnp.einsum("td,dcf->tcf", hidden_in, w_gate_up, preferred_element_type=jnp.float32)
    hidden = (gate_up[:, 0] * gate_up[:, 1]).astype(jnp.bfloat16)
    result = middle + scatter_rows(jnp.dot(hidden, w_down, preferred_element_type=jnp.float32))
    kept_parts = (token_rows, normed_full, chosen, slopes, logsum, prefix, mixed, middle, hidden_in)
    return (result, kept_parts)


def layer_backward(grad_rows, kept_parts, weights, decays, segments, section_first, glu_hook):
    token_rows, normed_full, chosen, slopes, logsum, prefix, mixed, middle, hidden_in = kept_parts
    w_qkv, w_out, w_gate_up, w_down, gain_pair = weights
    length = normed_full.shape[0]
    heads_local = chosen.shape[2]
    grad_branch = gather_grads(grad_rows.astype(jnp.bfloat16))
    gate_up = jnp.einsum("td,dcf->tcf", hidden_in, w_gate_up, preferred_element_type=jnp.float32)
    hidden = (gate_up[:, 0] * gate_up[:, 1]).astype(jnp.bfloat16)
    grad_down = jnp.einsum("tf,td->fd", hidden, grad_branch, preferred_element_type=jnp.float32)
    grad_hidden = jnp.einsum("td,fd->tf", grad_branch, w_down, preferred_element_type=jnp.float32)
    grad_gate_up = jnp.stack(
        [grad_hidden * gate_up[:, 1], grad_hidden * gate_up[:, 0]], axis=1
    ).astype(jnp.bfloat16)
    glu_grads = glu_hook(
        jnp.einsum("td,tcf->dcf", hidden_in, grad_gate_up, preferred_element_type=jnp.float32),
        grad_down,
    )
    grad_mid_normed = scatter_grads(
        jnp.einsum("tcf,dcf->td", grad_gate_up, w_gate_up, preferred_element_type=jnp.float32)
    )
    grad_middle, grad_gain_mid = rms_back(middle, rms_scale(middle), gain_pair[1], grad_mid_normed)
    grad_middle = grad_middle + grad_rows
    grad_attn = gather_grads(grad_middle.astype(jnp.bfloat16))
    grad_wout = jnp.einsum("tf,td->fd", mixed, grad_attn, preferred_element_type=jnp.float32)
    grad_mixed = jnp.einsum("td,fd->tf", grad_attn, w_out, preferred_element_type=jnp.float32)
    grad_mixed = grad_mixed.reshape(length // BLOCK, BLOCK, heads_local, HDIM)
    query_blocks, key_blocks, value_blocks, decay_blocks, segment_blocks = split_blocks(
        chosen, decays, segments
    )
    allowed = block_mask(segment_blocks)
    diag_parts = diag_backward(
        query_blocks, key_blocks, value_blocks, allowed, logsum, grad_mixed.astype(jnp.bfloat16)
    )
    norm_parts = norm_backward(
        query_blocks,
        key_blocks,
        value_blocks,
        decay_blocks,
        segment_blocks,
        allowed,
        prefix,
        grad_mixed,
    )
    diag_grads = jnp.stack(
        [member.reshape(length, heads_local, HDIM) for member in diag_parts], axis=1
    )
    norm_query = norm_parts[0].reshape(length, heads_local, HDIM) * slopes[:, 0]
    norm_keys = norm_parts[1].reshape(length, heads_local, HDIM) * slopes[:, 1]
    norm_grads = jnp.stack(
        [norm_query, norm_keys, norm_parts[2].reshape(length, heads_local, HDIM)], axis=1
    )
    grad_project = (
        jnp.where(section_first, diag_grads, norm_grads)
        .astype(jnp.bfloat16)
        .reshape(length, 3, heads_local * HDIM)
    )
    grad_wqkv = jnp.einsum(
        "td,tcf->dcf", normed_full, grad_project, preferred_element_type=jnp.float32
    )
    grad_in_normed = scatter_grads(
        jnp.einsum("tcf,dcf->td", grad_project, w_qkv, preferred_element_type=jnp.float32)
    )
    grad_input, grad_gain_in = rms_back(
        token_rows, rms_scale(token_rows), gain_pair[0], grad_in_normed
    )
    return (
        grad_input + grad_middle,
        (grad_wqkv, grad_wout),
        glu_grads,
        jnp.stack([grad_gain_in, grad_gain_mid]),
    )


def body(tokens, w_qkv, w_out, w_gate_up, w_down, norm_gains, log_decay, segment_ids, cotangent):
    section_count = lax.axis_size("section")
    section_index = lax.axis_index("section")
    section_first = section_index == 0
    section_final = section_index == section_count - 1
    micro_count = tokens.shape[0]
    step_count = micro_count + section_count - 1
    weights = (w_qkv[0], w_out[0], w_gate_up[0], w_down[0], norm_gains[0])
    segments_all = segment_ids.astype(jnp.float32)
    received = jnp.zeros(tokens.shape[1:], jnp.float32)
    layer_outs = jnp.zeros(tokens.shape, jnp.bfloat16)
    saved_tensors = None
    for moment in range(step_count):
        offset = moment - section_index
        active = (offset >= 0) & (offset < micro_count)
        micro_index = jnp.clip(offset, 0, micro_count - 1)
        own_rows = lax.dynamic_index_in_dim(tokens, micro_index, 0, keepdims=False).astype(
            jnp.float32
        )
        token_rows = jnp.where(section_first, own_rows, received)
        decays = lax.dynamic_index_in_dim(log_decay, micro_index, 0, keepdims=False)
        segments = lax.dynamic_index_in_dim(segments_all, micro_index, 0, keepdims=False)
        result, kept_parts = layer_forward(token_rows, weights, decays, segments, section_first)
        if saved_tensors is None:
            saved_tensors = jax.tree.map(
                lambda member: jnp.zeros((micro_count,) + member.shape, member.dtype), kept_parts
            )
        saved_tensors = jax.tree.map(
            lambda stacked, member: place_at(stacked, member, micro_index, active),
            saved_tensors,
            kept_parts,
        )
        sent_rows = result.astype(jnp.bfloat16)
        layer_outs = place_at(layer_outs, sent_rows, micro_index, active)
        if moment < step_count - 1:
            received = from_behind(sent_rows, "section", 1).astype(jnp.float32)
    received_back = jnp.zeros(tokens.shape[1:], jnp.float32)
    input_grads = jnp.zeros(tokens.shape, jnp.float32)
    total_qkv = jnp.zeros(w_qkv.shape[1:], jnp.float32)
    total_out = jnp.zeros(w_out.shape[1:], jnp.float32)
    total_gate_up = jnp.zeros(w_gate_up.shape[1:], jnp.float32)
    total_down = jnp.zeros(w_down.shape[1:], jnp.float32)
    total_gains = jnp.zeros(norm_gains.shape[1:], jnp.float32)
    for moment in range(step_count):
        offset = moment - (section_count - 1 - section_index)
        active = (offset >= 0) & (offset < micro_count)
        micro_index = jnp.clip(offset, 0, micro_count - 1)
        own_grads = lax.dynamic_index_in_dim(cotangent, micro_index, 0, keepdims=False).astype(
            jnp.float32
        )
        grad_rows = jnp.where(section_final, own_grads, received_back)
        kept_parts = jax.tree.map(
            lambda stacked: lax.dynamic_index_in_dim(stacked, micro_index, 0, keepdims=False),
            saved_tensors,
        )
        decays = lax.dynamic_index_in_dim(log_decay, micro_index, 0, keepdims=False)
        segments = lax.dynamic_index_in_dim(segments_all, micro_index, 0, keepdims=False)

        def glu_hook(grad_gate_up, grad_down):
            summed_gate_up = total_gate_up + jnp.where(active, grad_gate_up, 0.0)
            summed_down = total_down + jnp.where(active, grad_down, 0.0)
            return (summed_gate_up, summed_down)

        grad_input, mixer_grads, glu_grads, gain_grads = layer_backward(
            grad_rows, kept_parts, weights, decays, segments, section_first, glu_hook
        )
        total_gate_up, total_down = glu_grads
        total_qkv = total_qkv + jnp.where(active, mixer_grads[0], 0.0)
        total_out = total_out + jnp.where(active, mixer_grads[1], 0.0)
        total_gains = total_gains + jnp.where(active, gain_grads, 0.0)
        sent_back = grad_input.astype(jnp.bfloat16)
        input_grads = place_at(
            input_grads,
            jnp.where(section_first, grad_input, sent_back.astype(jnp.float32)),
            micro_index,
            active,
        )
        if moment < step_count - 1:
            received_back = from_behind(sent_back, "section", -1).astype(jnp.float32)
    total_qkv, total_out, total_gate_up, total_down = (
        lax.psum(total_qkv.astype(jnp.bfloat16), "seq").astype(jnp.float32),
        lax.psum(total_out.astype(jnp.bfloat16), "seq").astype(jnp.float32),
        lax.psum(total_gate_up.astype(jnp.bfloat16), "seq").astype(jnp.float32),
        lax.psum(total_down.astype(jnp.bfloat16), "seq").astype(jnp.float32),
    )
    total_gains = lax.psum(total_gains, ("seq", "tensor"))
    return (
        layer_outs[None],
        input_grads[None],
        total_qkv[None],
        total_out[None],
        total_gate_up[None],
        total_down[None],
        total_gains[None],
    )


def solution(mesh):
    return jax.shard_map(
        body,
        mesh=mesh,
        in_specs=(
            P(None, ("seq", "tensor"), None),
            P("section", None, None, "tensor"),
            P("section", "tensor", None),
            P("section", None, None, "tensor"),
            P("section", "tensor", None),
            P("section", None, None),
            P(None, "seq", "tensor"),
            P(None, "seq"),
            P(None, ("seq", "tensor"), None),
        ),
        out_specs=(
            P("section", None, ("seq", "tensor"), None),
            P("section", None, ("seq", "tensor"), None),
            P("section", None, None, "tensor"),
            P("section", "tensor", None),
            P("section", None, None, "tensor"),
            P("section", "tensor", None),
            P("section", None, None),
        ),
        check_vma=False,
    )
```

profile of v0, /device:TPU:0, one launch (start us, length us, event | category | flops | bytes accessed | tf_op | source)
XLA Modules:
  0.0 1646.4 jit_solution(135178551462116769)
XLA Ops:
  23.4 6.3 fusion.502
  42.1 9.1 all-reduce.18
  82.3 18.8 %while.237 = (s32[]{:T(128)}, f32[4,64,64]{2,1,0:T(8,128)S(1)}, f32[8,4,64,64]{3,2,1,0:T(8,128)}, f32[8,4]{1,0:T(8,128)}, f32[8,4,64,64]{3,2,1,0:T(8,128)}, /*index=5*/s32[]{:T(128)}, s32[]{:T(128)}) while((s32[]{:T(128)}, f32[4,64,64]{2,1,0:T(8,128)S(1)}, f32[8,4,64,64]{3,2,1,0:T(8,128)}, f32[8,4]{1,0:T(8,128)}, ...), condition=%wide.region_6.7_spmd.clone, body=%wide.region_5.6_spmd.clone.sunk | while | flops 65539 | bytes 393372 | solution.py:192
  101.2 6.4 all-gather.3
  107.6 16.5 %while.238 = (s32[]{:T(128)}, f32[]{:T(128)}, f32[4,64,64]{2,1,0:T(8,128)S(1)}, s32[]{:T(128)}, bf16[4]{0:T(256)(128)(2,1)S(1)}, /*index=5*/bf16[4,4]{1,0:T(4,12...) while((s32[]{:T(128)}, f32[]{:T(128)}, ...), condition=%wide.region_8.9_spmd.clone, body=%wide.region_7.8_spmd.clone.sunk | while | flops 81940 | bytes 164134 | solution.py:38
  139.4 27.5 %reduce-scatter.13.cloned.1.call-done = bf16[128,1024]{1,0:T(8,128)(2,1)} async-done(((bf16[512,1024]{1,0:T(8,128)(2,1)}), bf16[128,1024]{1,0:T(8,128)(2,1)}) %reduce-scatter.13.cloned.1.call-update) | async-done | bytes 262160 | tf_op jit(solution)/shard_map/reduce_scatter | solution.py:69
  169.9 26.7 %all-gather.33.cloned.1.call-done = bf16[512,1024]{1,0:T(8,128)(2,1)} async-done(((bf16[128,1024]{1,0:T(8,128)(2,1)}), bf16[512,1024]{1,0:T(8,128)(2,1)}) %all-gather.33.cloned.1.call-update) | async-done | bytes 1048592 | tf_op jit(solution)/shard_map/all_gather | solution.py:65
  201.8 26.7 %reduce-scatter.15.cloned.1.call-done = bf16[128,1024]{1,0:T(8,128)(2,1)} async-done(((bf16[512,1024]{1,0:T(8,128)(2,1)}), bf16[128,1024]{1,0:T(8,128)(2,1)}) %reduce-scatter.15.cloned.1.call-update) | async-done | bytes 262160 | tf_op jit(solution)/shard_map/reduce_scatter | solution.py:69
  230.5 3.4 collective-permute-start
  233.9 5.4 collective-permute-done
  250.3 18.5 %all-gather.35.cloned.1.call-done = bf16[512,1024]{1,0:T(8,128)(2,1)} async-done(((bf16[128,1024]{1,0:T(8,128)(2,1)}), bf16[512,1024]{1,0:T(8,128)(2,1)}) %all-gather.35.cloned.1.call-update) | async-done | bytes 1048592 | tf_op jit(solution)/shard_map/all_gather | solution.py:65
  289.9 35.7 %while.239 = (s32[]{:T(128)}, f32[4,64,64]{2,1,0:T(8,128)}, f32[8,4,64,64]{3,2,1,0:T(8,128)}, f32[8,4]{1,0:T(8,128)}, f32[8,4,64,64]{3,2,1,0:T(8,128)}, /*index=5*/s32[]{:T(128)}, s32[]{:T(128)}) while((s32[]{:T(128)}, f32[4,64,64]{2,1,0:T(8,128)}, f32[8,4,64,64]{3,2,1,0:T(8,128)}, f32[8,4]{1,0:T(8,128)}, ...), condition=%wide.region_20.21_spmd.clone, body=%wide.region_19.20_spmd.clone.sunk | while | flops 65539 | bytes 524444 | solution.py:192
  326.5 6.2 all-gather.7
  332.8 27.1 %while.240 = (s32[]{:T(128)}, f32[]{:T(128)}, f32[4,64,64]{2,1,0:T(8,128)}, s32[]{:T(128)}, bf16[4]{0:T(256)(128)(2,1)}, /*index=5*/bf16[4,4]{1,0:T(4,128)(2,1)}...) while((s32[]{:T(128)}, f32[]{:T(128)}, ...), condition=%wide.region_22.23_spmd.clone, body=%wide.region_21.22_spmd.clone.sunk | while | flops 81940 | bytes 164134 | solution.py:38
  383.1 26.8 %reduce-scatter.17.cloned.1.call-done = bf16[128,1024]{1,0:T(8,128)(2,1)} async-done(((bf16[512,1024]{1,0:T(8,128)(2,1)}), bf16[128,1024]{1,0:T(8,128)(2,1)}) %reduce-scatter.17.cloned.1.call-update) | async-done | bytes 262160 | tf_op jit(solution)/shard_map/reduce_scatter | solution.py:69
  413.5 26.2 %all-gather.37.cloned.1.call-done = bf16[512,1024]{1,0:T(8,128)(2,1)} async-done(((bf16[128,1024]{1,0:T(8,128)(2,1)}), bf16[512,1024]{1,0:T(8,128)(2,1)}) %all-gather.37.cloned.1.call-update) | async-done | bytes 1048592 | tf_op jit(solution)/shard_map/all_gather | solution.py:65
  446.6 25.0 %reduce-scatter.19.cloned.1.call-done = bf16[128,1024]{1,0:T(8,128)(2,1)} async-done(((bf16[512,1024]{1,0:T(8,128)(2,1)}), bf16[128,1024]{1,0:T(8,128)(2,1)}) %reduce-scatter.19.cloned.1.call-update) | async-done | bytes 262160 | tf_op jit(solution)/shard_map/reduce_scatter | solution.py:69
  473.8 3.4 collective-permute-start.1
  477.1 5.4 collective-permute-done.1
  495.3 16.8 %all-gather.39.cloned.1.call-done = bf16[512,1024]{1,0:T(8,128)(2,1)} async-done(((bf16[128,1024]{1,0:T(8,128)(2,1)}), bf16[512,1024]{1,0:T(8,128)(2,1)}) %all-gather.39.cloned.1.call-update) | async-done | bytes 1048592 | tf_op jit(solution)/shard_map/all_gather | solution.py:65
  533.2 35.1 %while.241 = (s32[]{:T(128)}, f32[4,64,64]{2,1,0:T(8,128)}, f32[8,4,64,64]{3,2,1,0:T(8,128)}, f32[8,4]{1,0:T(8,128)}, f32[8,4,64,64]{3,2,1,0:T(8,128)}, /*index=5*/s32[]{:T(128)}, s32[]{:T(128)}) while((s32[]{:T(128)}, f32[4,64,64]{2,1,0:T(8,128)}, f32[8,4,64,64]{3,2,1,0:T(8,128)}, f32[8,4]{1,0:T(8,128)}, ...), condition=%wide.region_34.35_spmd.clone, body=%wide.region_33.34_spmd.clone.sunk | while | flops 65539 | bytes 524444 | solution.py:192
  569.2 6.4 all-gather.11
  575.6 26.8 %while.242 = (s32[]{:T(128)}, f32[]{:T(128)}, f32[4,64,64]{2,1,0:T(8,128)}, s32[]{:T(128)}, bf16[4]{0:T(256)(128)(2,1)}, /*index=5*/bf16[4,4]{1,0:T(4,128)(2,1)}...) while((s32[]{:T(128)}, f32[]{:T(128)}, ...), condition=%wide.region_36.37_spmd.clone, body=%wide.region_35.36_spmd.clone.sunk | while | flops 81940 | bytes 164134 | solution.py:38
  625.7 26.8 %reduce-scatter.21.cloned.1.call-done = bf16[128,1024]{1,0:T(8,128)(2,1)} async-done(((bf16[512,1024]{1,0:T(8,128)(2,1)}), bf16[128,1024]{1,0:T(8,128)(2,1)}) %reduce-scatter.21.cloned.1.call-update) | async-done | bytes 262160 | tf_op jit(solution)/shard_map/reduce_scatter | solution.py:69
  723.6 4.5 fusion.32
  728.1 3.5 fusion.182
  736.7 31.1 %while.243 = (s32[]{:T(128)}, f32[4,64,64]{2,1,0:T(8,128)}, f32[8,4,64,64]{3,2,1,0:T(8,128)}, f32[8,4]{1,0:T(8,128)}, f32[8,4,64,64]{3,2,1,0:T(8,128)}, /*index=5*/s32[]{:T(128)}, s32[]{:T(128)}) while((s32[]{:T(128)}, f32[4,64,64]{2,1,0:T(8,128)}, f32[8,4,64,64]{3,2,1,0:T(8,128)}, f32[8,4]{1,0:T(8,128)}, ...), condition=%wide.region_49.50_spmd.clone, body=%wide.region_48.49_spmd.clone.sunk | while | flops 65539 | bytes 524444 | solution.py:192
  793.4 3.7 dynamic-slice_bitcast_fusion
  801.1 16.0 all-gather.45.cloned.1.call-done
  842.3 35.7 %while.244 = (s32[]{:T(128)}, f32[4,64,64]{2,1,0:T(8,128)}, f32[4]{0:T(128)}, f32[8,4,64,64]{3,2,1,0:T(8,128)}, f32[8,4]{1,0:T(8,128)S(1)}, /*index=5*/f32[8,4,6...) while((s32[]{:T(128)}, f32[4,64,64]{2,1,0:T(8,128)}, f32[4]{0:T(128)}, ...), condition=%wide.region_54.55_spmd.clone, body=%wide.region_53.54_spmd.clone.sunk | while | flops 65548 | bytes 524565 | solution.py:286
  878.9 6.2 all-gather.12
  888.1 7.2 all-reduce.15
  895.4 6.5 while.245
  902.0 3.3 fusion.99
  928.0 24.6 %reduce-scatter.27.cloned.1.call-done = bf16[128,1024]{1,0:T(8,128)(2,1)} async-done(((bf16[512,1024]{1,0:T(8,128)(2,1)}), bf16[128,1024]{1,0:T(8,128)(2,1)}) %reduce-scatter.27.cloned.1.call-update) | async-done | bytes 262160 | tf_op jit(solution)/shard_map/reduce_scatter | solution.py:79
  958.8 8.5 collective-permute-done.2
  970.4 4.5 fusion.28
  974.9 19.9 %all-gather.47.cloned.1.call-done = bf16[512,1024]{1,0:T(8,128)(2,1)} async-done(((bf16[128,1024]{1,0:T(8,128)(2,1)}), bf16[512,1024]{1,0:T(8,128)(2,1)}) %all-gather.47.cloned.1.call-update) | async-done | bytes 1048592 | tf_op jit(solution)/shard_map/all_gather | solution.py:75
  994.8 3.5 fusion.184
  1023.0 6.0 reduce-scatter.29.cloned.1.call-done
  1035.2 35.1 %while.246 = (s32[]{:T(128)}, f32[4,64,64]{2,1,0:T(8,128)}, f32[8,4,64,64]{3,2,1,0:T(8,128)}, f32[8,4]{1,0:T(8,128)}, f32[8,4,64,64]{3,2,1,0:T(8,128)}, /*index=5*/s32[]{:T(128)}, s32[]{:T(128)}) while((s32[]{:T(128)}, f32[4,64,64]{2,1,0:T(8,128)}, f32[8,4,64,64]{3,2,1,0:T(8,128)}, f32[8,4]{1,0:T(8,128)}, ...), condition=%wide.region_66.67_spmd.clone, body=%wide.region_65.66_spmd.clone.sunk | while | flops 65539 | bytes 524444 | solution.py:192
  1108.0 45.6 %while.247 = (s32[]{:T(128)}, f32[4,64,64]{2,1,0:T(8,128)}, f32[4]{0:T(128)}, f32[8,4,64,64]{3,2,1,0:T(8,128)}, f32[8,4]{1,0:T(8,128)}, /*index=5*/f32[8,4,64,64...) while((s32[]{:T(128)}, f32[4,64,64]{2,1,0:T(8,128)}, f32[4]{0:T(128)}, ...), condition=%wide.region_71.72_spmd.clone, body=%wide.region_70.71_spmd.clone.sunk | while | flops 65548 | bytes 524565 | solution.py:286
  1154.6 6.2 all-gather.14
  1163.7 7.2 all-reduce.16
  1171.0 6.6 while.248
  1177.6 3.4 fusion.96
  1237.9 4.7 collective-permute-done.3
  1256.3 3.4 fusion.24
  1259.7 10.8 all-gather.51.cloned.1.call-done
  1270.5 3.5 fusion.186
  1279.1 31.1 %while.249 = (s32[]{:T(128)}, f32[4,64,64]{2,1,0:T(8,128)}, f32[8,4,64,64]{3,2,1,0:T(8,128)}, f32[8,4]{1,0:T(8,128)}, f32[8,4,64,64]{3,2,1,0:T(8,128)}, /*index=5*/s32[]{:T(128)}, s32[]{:T(128)}) while((s32[]{:T(128)}, f32[4,64,64]{2,1,0:T(8,128)}, f32[8,4,64,64]{3,2,1,0:T(8,128)}, f32[8,4]{1,0:T(8,128)}, ...), condition=%wide.region_83.84_spmd.clone, body=%wide.region_82.83_spmd.clone.sunk | while | flops 65539 | bytes 524444 | solution.py:192
  1333.3 4.1 fusion.131
  1341.5 4.7 fusion.188
  1349.2 4.2 fusion.128
  1383.8 45.3 %while.250 = (s32[]{:T(128)}, f32[4,64,64]{2,1,0:T(8,128)}, f32[4]{0:T(128)}, f32[8,4,64,64]{3,2,1,0:T(8,128)}, f32[8,4]{1,0:T(8,128)}, /*index=5*/f32[8,4,64,64...) while((s32[]{:T(128)}, f32[4,64,64]{2,1,0:T(8,128)}, f32[4]{0:T(128)}, ...), condition=%wide.region_88.89_spmd.clone, body=%wide.region_87.88_spmd.clone.sunk | while | flops 65548 | bytes 524565 | solution.py:286
  1430.0 6.4 all-gather.16
  1439.4 7.0 all-reduce.17
  1446.5 6.5 while.251
  1453.0 3.7 fusion.69
  1479.0 5.3 fusion.56
  1484.3 6.5 fusion.21
  1506.5 32.7 %psum.39 = f32[1,2,1024]{2,1,0:T(2,128)} all-reduce(f32[1,2,1024]{2,1,0:T(2,128)S(1)} %fusion.421), channel_id=1, replica_groups=mesh['section'=2,'seq'=4,'tensor'=4] {'seq','tensor'}, use_global_device_ids=true, to_apply=%region_103.104 | all-reduce | flops 2048 | bytes 16384 | tf_op jit(solution)/shard_map/psum | solution.py:514
  1541.5 88.1 %all-reduce.22.cloned.1.call-done = (bf16[1,1024,3,256]{3,1,2,0:T(8,128)(2,1)}, bf16[1,256,1024]{2,1,0:T(8,128)(2,1)}, bf16[1,1024,2,704]{1,3,2,0:T(8,128)(2,1)}, bf16[1,704,1024]{2,1,0:T(8,128)(2,1)}) async-done(((bf16[1,1024,3,256]{3,1,2,0:T(8,128)(2,1)}, bf16[1,256,1024]{2,1,0:T(8,128)(2,1)}, bf16[1,1024,2,704]{1,3,2,0:T(8,128)(2,1)}, bf16[1,704,1024]{2,1,0:T(8,128)(2,1)}), ...) | async-done | bytes 6422544 | tf_op jit(solution)/shard_map/psum | solution.py:509
  1629.7 3.5 broadcast_in_dim.594
  (1512 shorter events, 1004.6 us)
Async XLA Ops:
  7.2 189.4 %copy-start = (bf16[1,1024,2,704]{1,3,2,0:T(8,128)(2,1)S(1)}, bf16[1,1024,2,704]{1,3,2,0:T(8,128)(2,1)}, u32[]{:S(2)}) copy-start(bf16[1,1024,2,704]{1,3,2,0:T(8,128)(2,1)} %param.42) | copy-start | bytes 8650756
  7.2 28.4 %copy-start.252 = (u32[32]{0:T(128)S(1)}, u32[32]{0:T(128)}, u32[]{:S(2)}) copy-start(u32[32]{0:T(128)} %constant.812) | copy-start | bytes 388
  7.2 54.0 %all-gather.31.cloned.1.call-start = ((), (), s32[]{:S(2)}) async-start(), calls=%async_computation.12 | async-start | bytes 1310720 | tf_op jit(solution)/shard_map/all_gather | solution.py:65
  11.0 155.9 %reduce-scatter.13.cloned.1.call-start = ((), (), s32[]{:S(2)}) async-start(), calls=%async_computation.13 | async-start | bytes 1310720 | tf_op jit(solution)/shard_map/reduce_scatter | solution.py:69
  31.7 19.5 %copy-start.87 = (f32[8,64,4]{2,0,1:T(8,128)}, f32[8,64,4]{2,0,1:T(8,128)S(1)}, u32[]{:S(2)}) copy-start(f32[8,64,4]{2,0,1:T(8,128)S(1)} %fusion.504) | copy-start | bytes 24580
  82.3 25.3 %copy-start.228 = (bf16[4,4]{1,0:T(4,128)(2,1)S(1)}, bf16[4,4]{1,0:T(4,128)(2,1)}, u32[]{:S(2)}) copy-start(bf16[4,4]{1,0:T(4,128)(2,1)} %reshape.1173) | copy-start | bytes 100
  82.3 25.3 %copy-start.250 = (bf16[4]{0:T(256)(128)(2,1)S(1)}, bf16[4]{0:T(256)(128)(2,1)}, u32[]{:S(2)}) copy-start(bf16[4]{0:T(256)(128)(2,1)} %get-tuple-element.3026) | copy-start | bytes 28
  82.3 25.3 %copy-start.251 = (bf16[4]{0:T(256)(128)(2,1)S(1)}, bf16[4]{0:T(256)(128)(2,1)}, u32[]{:S(2)}) copy-start(bf16[4]{0:T(256)(128)(2,1)} %get-tuple-element.3028) | copy-start | bytes 28
  101.1 23.2 %copy-start.232 = (f32[8]{0:T(128)S(1)}, f32[8]{0:T(128)}, u32[]{:S(2)}) copy-start(f32[8]{0:T(128)} %copy-done.231) | copy-start | bytes 100
  101.1 23.5 %copy-start.244 = (f32[7]{0:T(128)S(1)}, f32[7]{0:T(128)}, u32[]{:S(2)}) copy-start(f32[7]{0:T(128)} %get-tuple-element.2427) | copy-start | bytes 88
  134.6 32.3 %copy-start.5 = (bf16[2,128,1024]{2,1,0:T(8,128)(2,1)S(1)}, bf16[2,128,1024]{2,1,0:T(8,128)(2,1)}, u32[]{:S(2)}) copy-start(bf16[2,128,1024]{2,1,0:T(8,128)(2,1)} %param.39) | copy-start | bytes 1572868
  139.3 57.3 %all-gather.33.cloned.1.call-start = ((), (), s32[]{:S(2)}) async-start(), calls=%async_computation.14 | async-start | bytes 1310720 | tf_op jit(solution)/shard_map/all_gather | solution.py:65
  169.8 58.6 %reduce-scatter.15.cloned.1.call-start = ((), (), s32[]{:S(2)}) async-start(), calls=%async_computation.15 | async-start | bytes 1310720 | tf_op jit(solution)/shard_map/reduce_scatter | solution.py:69
  201.7 39.5 %copy-start.226 = (f32[8,1,4]{2,0,1:T(8,128)S(1)}, f32[8,1,4]{2,0,1:T(8,128)}, u32[]{:S(2)}) copy-start(f32[8,1,4]{2,0,1:T(8,128)} %get-tuple-element.2334) | copy-start | bytes 388
  201.7 39.6 %copy-start.209 = (f32[7,1]{1,0:T(8,128)S(1)}, f32[7,1]{1,0:T(8,128)}, u32[]{:S(2)}) copy-start(f32[7,1]{1,0:T(8,128)} %get-tuple-element.2370) | copy-start | bytes 88
  201.7 44.2 %copy-start.249 = (bf16[16]{0:T(256)(128)(2,1)S(1)}, bf16[16]{0:T(256)(128)(2,1)}, u32[]{:S(2)}) copy-start(bf16[16]{0:T(256)(128)(2,1)} %get-tuple-element.2247) | copy-start | bytes 100
  201.7 67.1 %all-gather.35.cloned.1.call-start = ((), (), s32[]{:S(2)}) async-start(), calls=%async_computation.16 | async-start | bytes 1310720 | tf_op jit(solution)/shard_map/all_gather | solution.py:65
  230.5 8.7 collective-permute-start
  240.8 169.0 %reduce-scatter.17.cloned.1.call-start = ((), (), s32[]{:S(2)}) async-start(), calls=%async_computation.17 | async-start | bytes 1310720 | tf_op jit(solution)/shard_map/reduce_scatter | solution.py:69
  241.3 30.3 %copy-start.214 = (f32[8,1,4]{0,2,1:T(4,128)}, f32[8,1,4]{0,2,1:T(4,128)S(1)}, u32[]{:S(2)}) copy-start(f32[8,1,4]{0,2,1:T(4,128)S(1)} %copy.988) | copy-start | bytes 388
  359.9 14.2 copy-start.76
  383.0 56.7 %all-gather.37.cloned.1.call-start = ((), (), s32[]{:S(2)}) async-start(), calls=%async_computation.18 | async-start | bytes 1310720 | tf_op jit(solution)/shard_map/all_gather | solution.py:65
  413.0 58.6 %reduce-scatter.19.cloned.1.call-start = ((), (), s32[]{:S(2)}) async-start(), calls=%async_computation.19 | async-start | bytes 1310720 | tf_op jit(solution)/shard_map/reduce_scatter | solution.py:69
  444.8 39.3 %copy-start.224 = (f32[8,1,4]{2,0,1:T(8,128)S(1)}, f32[8,1,4]{2,0,1:T(8,128)}, u32[]{:S(2)}) copy-start(f32[8,1,4]{2,0,1:T(8,128)} %get-tuple-element.2421) | copy-start | bytes 388
  444.9 39.4 %copy-start.194 = (f32[8,64]{1,0:T(8,128)S(1)}, f32[8,64]{1,0:T(8,128)}, u32[]{:S(2)}) copy-start(f32[8,64]{1,0:T(8,128)} %copy-done.193) | copy-start | bytes 6148
  444.9 67.2 %all-gather.39.cloned.1.call-start = ((), (), s32[]{:S(2)}) async-start(), calls=%async_computation.20 | async-start | bytes 1310720 | tf_op jit(solution)/shard_map/all_gather | solution.py:65
  446.6 44.2 %copy-start.248 = (bf16[16]{0:T(256)(128)(2,1)S(1)}, bf16[16]{0:T(256)(128)(2,1)}, u32[]{:S(2)}) copy-start(bf16[16]{0:T(256)(128)(2,1)} %get-tuple-element.2250) | copy-start | bytes 100
  473.8 8.8 collective-permute-start.1
  484.1 168.4 %reduce-scatter.21.cloned.1.call-start = ((), (), s32[]{:S(2)}) async-start(), calls=%async_computation.21 | async-start | bytes 1310720 | tf_op jit(solution)/shard_map/reduce_scatter | solution.py:69
  484.2 30.5 %copy-start.213 = (f32[8,1,4]{0,2,1:T(4,128)}, f32[8,1,4]{0,2,1:T(4,128)S(1)}, u32[]{:S(2)}) copy-start(f32[8,1,4]{0,2,1:T(4,128)S(1)} %copy.1011) | copy-start | bytes 388
  602.5 14.2 copy-start.74
  625.7 95.3 %all-gather.41.cloned.1.call-start = ((), (), s32[]{:S(2)}) async-start(), calls=%async_computation.22 | async-start | bytes 1310720 | tf_op jit(solution)/shard_map/all_gather | solution.py:65
  655.6 72.5 %all-gather.43.cloned.1.call-start = ((), (), s32[]{:S(2)}) async-start(), calls=%async_computation.24 | async-start | bytes 1310720 | tf_op jit(solution)/shard_map/all_gather | solution.py:75
  657.4 128.3 %reduce-scatter.25.cloned.1.call-start = ((), (), s32[]{:S(2)}) async-start(), calls=%async_computation.25 | async-start | bytes 1310720 | tf_op jit(solution)/shard_map/reduce_scatter | solution.py:79
  658.0 15.5 copy-start.73
  735.5 81.5 %all-gather.45.cloned.1.call-start = ((), (), s32[]{:S(2)}) async-start(), calls=%async_computation.26 | async-start | bytes 1310720 | tf_op jit(solution)/shard_map/all_gather | solution.py:75
  736.7 31.1 %copy-start.215 = (f32[8,4]{0,1:T(4,128)S(1)}, f32[8,4]{0,1:T(4,128)}, u32[]{:S(2)}) copy-start(f32[8,4]{0,1:T(4,128)} %get-tuple-element.2383) | copy-start | bytes 388
  790.0 162.6 %reduce-scatter.27.cloned.1.call-start = ((), (), s32[]{:S(2)}) async-start(), calls=%async_computation.27 | async-start | bytes 1310720 | tf_op jit(solution)/shard_map/reduce_scatter | solution.py:79
  801.0 18.6 %copy-start.152 = (f32[8,4,64]{2,1,0:T(4,128)S(1)}, f32[8,4,64]{2,1,0:T(4,128)}, u32[]{:S(2)}) copy-start(f32[8,4,64]{2,1,0:T(4,128)} %get-tuple-element.2340) | copy-start | bytes 24580
  878.0 23.9 %copy-start.146 = (f32[8,64,4]{1,2,0:T(4,128)S(1)}, f32[8,64,4]{1,2,0:T(4,128)}, u32[]{:S(2)}) copy-start(f32[8,64,4]{1,2,0:T(4,128)} %copy-done.145) | copy-start | bytes 24580
  926.8 28.3 %copy-start.230 = (f32[128]{0:T(128)S(1)}, f32[128]{0:T(128)}, u32[]{:S(2)}) copy-start(f32[128]{0:T(128)} %copy-done.229) | copy-start | bytes 1540
  926.8 28.3 %copy-start.237 = (f32[128]{0:T(128)S(1)}, f32[128]{0:T(128)}, u32[]{:S(2)}) copy-start(f32[128]{0:T(128)} %copy-done.236) | copy-start | bytes 1540
  926.8 68.0 %all-gather.47.cloned.1.call-start = ((), (), s32[]{:S(2)}) async-start(), calls=%async_computation.28 | async-start | bytes 1310720 | tf_op jit(solution)/shard_map/all_gather | solution.py:75
  955.0 13.0 copy-start.68
  955.2 13.7 copy-start.192
  955.2 14.3 copy-start.212
  957.5 9.8 collective-permute-start.2
  968.8 60.3 %reduce-scatter.29.cloned.1.call-start = ((), (), s32[]{:S(2)}) async-start(), calls=%async_computation.29 | async-start | bytes 1310720 | tf_op jit(solution)/shard_map/reduce_scatter | solution.py:79
  1002.2 80.0 %all-gather.49.cloned.1.call-start = ((), (), s32[]{:S(2)}) async-start(), calls=%async_computation.30 | async-start | bytes 1310720 | tf_op jit(solution)/shard_map/all_gather | solution.py:75
  1017.7 13.5 copy-start.147
  1033.7 194.0 %reduce-scatter.31.cloned.1.call-start = ((), (), s32[]{:S(2)}) async-start(), calls=%async_computation.31 | async-start | bytes 1310720 | tf_op jit(solution)/shard_map/reduce_scatter | solution.py:79
  1153.6 24.0 %copy-start.148 = (f32[8,64,4]{1,2,0:T(4,128)S(1)}, f32[8,64,4]{1,2,0:T(4,128)}, u32[]{:S(2)}) copy-start(f32[8,64,4]{1,2,0:T(4,128)} %copy-done.147) | copy-start | bytes 24580
  1153.6 24.0 %copy-start.208 = (f32[8,4]{1,0:T(8,128)S(1)}, f32[8,4]{1,0:T(8,128)}, u32[]{:S(2)}) copy-start(f32[8,4]{1,0:T(8,128)} %get-tuple-element.1440) | copy-start | bytes 388
  1202.6 67.9 %all-gather.51.cloned.1.call-start = ((), (), s32[]{:S(2)}) async-start(), calls=%async_computation.32 | async-start | bytes 1310720 | tf_op jit(solution)/shard_map/all_gather | solution.py:75
  1232.5 10.1 collective-permute-start.3
  1244.5 79.8 %reduce-scatter.33.cloned.1.call-start = ((), (), s32[]{:S(2)}) async-start(), calls=%async_computation.33 | async-start | bytes 1310720 | tf_op jit(solution)/shard_map/reduce_scatter | solution.py:79
  1277.9 83.2 %all-gather.53.cloned.1.call-start = ((), (), s32[]{:S(2)}) async-start(), calls=%async_computation.34 | async-start | bytes 1310720 | tf_op jit(solution)/shard_map/all_gather | solution.py:75
  1318.5 52.0 %copy-start.149 = (f32[8,64,4]{1,2,0:T(4,128)}, f32[8,64,4]{1,2,0:T(4,128)S(1)}, u32[]{:S(2)}) copy-start(f32[8,64,4]{1,2,0:T(4,128)S(1)} %copy.1151) | copy-start | bytes 24580
  1328.7 170.6 %reduce-scatter.23.cloned.1.call-start = ((), (), s32[]{:S(2)}) async-start(), calls=%async_computation.23 | async-start | bytes 1310720 | tf_op jit(solution)/shard_map/reduce_scatter | solution.py:69
  1341.2 163.8 %reduce-scatter.35.cloned.1.call-start = ((), (), s32[]{:S(2)}) async-start(), calls=%async_computation.35 | async-start | bytes 1310720 | tf_op jit(solution)/shard_map/reduce_scatter | solution.py:79
  1429.1 23.9 %copy-start.144 = (f32[8,64,4]{1,2,0:T(4,128)S(1)}, f32[8,64,4]{1,2,0:T(4,128)}, u32[]{:S(2)}) copy-start(f32[8,64,4]{1,2,0:T(4,128)} %copy-done.143) | copy-start | bytes 24580
  1429.1 23.9 %copy-start.207 = (f32[8,4]{1,0:T(8,128)S(1)}, f32[8,4]{1,0:T(8,128)}, u32[]{:S(2)}) copy-start(f32[8,4]{1,0:T(8,128)} %get-tuple-element.1446) | copy-start | bytes 388
  1478.7 151.0 %all-reduce.22.cloned.1.call-start = ((), (), s32[]{:S(2)}) async-start(), calls=%async_computation.36 | async-start | bytes 12845056 | tf_op jit(solution)/shard_map/psum | solution.py:509
  1501.5 37.7 %copy-start.114 = (f32[128,1024]{1,0:T(8,128)S(1)}, f32[128,1024]{1,0:T(8,128)}, u32[]{:S(2)}) copy-start(f32[128,1024]{1,0:T(8,128)} %get-tuple-element.2263) | copy-start | bytes 1572868
  (232 other events, 751.2 us)
Sparse Core Ops, SparseCore 0:
  11.2 30.6 all-gather.30
  139.4 27.4 reduce-scatter.12
  170.0 26.5 all-gather.32
  201.8 26.6 reduce-scatter.14
  241.0 27.7 all-gather.34
  383.2 26.6 reduce-scatter.16
  413.1 26.5 all-gather.36
  445.0 26.6 reduce-scatter.18
  484.2 27.7 all-gather.38
  625.8 26.6 reduce-scatter.20
  655.7 26.5 all-gather.40
  683.9 27.4 all-gather.42
  735.6 26.0 reduce-scatter.24
  790.2 26.8 all-gather.44
  926.9 25.7 reduce-scatter.26
  968.9 25.8 all-gather.46
  1002.4 26.6 reduce-scatter.28
  1033.8 26.6 all-gather.48
  1202.7 24.9 reduce-scatter.30
  1244.6 25.8 all-gather.50
  1278.0 26.6 reduce-scatter.32
  1328.8 27.4 all-gather.52
  1359.1 26.6 reduce-scatter.22
  1478.8 26.1 reduce-scatter.34
  1508.2 121.4 all-reduce.21
where the time goes:
time: 1670 us; the launch traced here: 1650 us
  local copies, waits for them, and re-layouts  454 us (27%)
  waiting for transfers between devices  416 us (25%)
  other arithmetic  392 us (23%)
  matrix products  218 us (13%)
  blocking collectives  101 us (6%)
  between operations  27.6 us (2%)
  loops' own time  24.2 us (1%)
    reduce_scatter x6, waiting for transfers between devices, scatter_rows(): lax.psum_scatter(partial_sum.astype(jnp.bfloat16), 'tensor', scatter_dime...  133 us
    psum x1, waiting for transfers between devices, body(): lax.psum(total_qkv.astype(jnp.bfloat16), 'seq').astype(jnp.float32)  88.1 us
    all_gather x6, waiting for transfers between devices, gather_rows(): return lax.all_gather(shard_piece, 'tensor', axis=0, tiled=True)  88.1 us
    add x48, other arithmetic, advance(): return (element[0][:, None, None] * state + element[1], state)  73.3 us
    while x64, local copies, waits for them, and re-layouts  57.9 us
    unnamed x577, local copies, waits for them, and re-layouts  51.4 us
    dynamic_update_slice x72, other arithmetic, norm_local(): lax.scan(advance, jnp.zeros(block_states.shape[1:], jnp.float32), (intern...  47.9 us
    all_gather x7, blocking collectives, carried_in(): lax.all_gather(part.astype(kind), axis)  47.1 us
  transfers between devices with their start and end apart: 29, of which 21 were waited for; matrix products, arithmetic and copies ran while one was open for 30% of the time, Pallas kernels for 0%

commit v1 on v0

v1 whole, which is shorter than its diff:
```python
import functools

import jax
import jax.numpy as jnp
from jax import lax
from jax.experimental import pallas as pl
from jax.experimental.pallas import tpu as pltpu
from jax.sharding import PartitionSpec as P

HDIM = 64
BLOCK = 64
PAIR = 2 * HDIM
TILE = 256

epsilon = 1e-05
head_epsilon = 1.0
far_below = -1e30

F32 = jnp.float32
BF16 = jnp.bfloat16
vmem_limit = 56 * 1024 * 1024


def nn(a, b):
    return lax.dot_general(a, b, (((1,), (0,)), ((), ())), preferred_element_type=F32)


def nt(a, b):
    return lax.dot_general(a, b, (((1,), (1,)), ((), ())), preferred_element_type=F32)


def tn(a, b):
    return lax.dot_general(a, b, (((0,), (0,)), ((), ())), preferred_element_type=F32)


def tiles(extent):
    return [(at, min(TILE, extent - at)) for at in range(0, extent, TILE)]


def low_lanes(rows):
    return lax.broadcasted_iota(jnp.int32, (rows, PAIR), 1) < HDIM


def lane_masks(rows):
    low = low_lanes(rows)
    one = jnp.where(low, 1.0, 0.0)
    return low, one.astype(BF16), (1.0 - one).astype(BF16)


def stack2(pair, masks):
    return jnp.concatenate([pair * masks[1], pair * masks[2]], axis=0)


def pick(stacked, masks):
    rows = stacked.shape[0] // 2
    return jnp.where(masks[0], stacked[:rows], stacked[rows:])


def spread2(columns, at, masks):
    return jnp.where(masks[0], columns[:, at : at + 1], columns[:, at + 1 : at + 2])


def block_diagonal():
    rows = lax.broadcasted_iota(jnp.int32, (PAIR, PAIR), 0) < HDIM
    lanes = lax.broadcasted_iota(jnp.int32, (PAIR, PAIR), 1) < HDIM
    return rows == lanes


def by_rows(first, second):
    rows = lax.broadcasted_iota(jnp.int32, (PAIR, PAIR), 0) < HDIM
    return jnp.where(rows, first, second)


def pack_states(first, second):
    lanes = lax.broadcasted_iota(jnp.int32, (PAIR, PAIR), 1) < HDIM
    return jnp.where(
        lanes, first + pltpu.roll(first, HDIM, 1), second + pltpu.roll(second, HDIM, 1)
    )


def unpack_states(packed):
    lanes = lax.broadcasted_iota(jnp.int32, (PAIR, PAIR), 1) < HDIM
    turned = pltpu.roll(packed, HDIM, 1)
    mask = block_diagonal()
    return (
        jnp.where(mask, jnp.where(lanes, packed, turned), 0.0),
        jnp.where(mask, jnp.where(lanes, turned, packed), 0.0),
    )


def chain_sum(every, weights, which, heads):
    count = every.shape[0] // PAIR
    rows = lax.broadcasted_iota(jnp.int32, (PAIR, PAIR), 0) < HDIM
    lanes = lax.broadcasted_iota(jnp.int32, (PAIR, PAIR), 1) < HDIM

    def lap(at, total):
        base = (which * count + at) * heads
        weight = jnp.where(
            rows,
            jnp.where(lanes, weights[base], weights[base + 2]),
            jnp.where(lanes, weights[base + 1], weights[base + 3]),
        )
        start = pl.multiple_of(at * PAIR, PAIR)
        return total + weight * every[pl.ds(start, PAIR), :].astype(F32)

    return lax.fori_loop(0, count, lap, jnp.zeros((PAIR, PAIR), F32))


def stacked_position(rows):
    shape = (2 * rows, rows)
    at = lax.broadcasted_iota(jnp.int32, shape, 0)
    return (
        jnp.where(at >= rows, at - rows, at),
        lax.broadcasted_iota(jnp.int32, shape, 1),
        at < rows,
    )


def same_segment(columns, rows_meta, heads):
    seg = columns[:, heads : heads + 1]
    return jnp.concatenate([seg, seg], axis=0) == rows_meta[heads : heads + 1, :]


def load_start(flags, layer, sources, target, sem):
    own, own_far, own_near, other_far, other_near = sources
    half = target.shape[0] // 2
    mine, home, upper = (flags[0] == layer, flags[2] == 1, flags[1])
    far = target.at[pl.ds(pl.multiple_of(upper * half, half), half), :]
    near = target.at[pl.ds(pl.multiple_of((1 - upper) * half, half), half), :]

    @pl.when(mine & home)
    def _():
        pltpu.make_async_copy(own, target, sem).start()

    @pl.when(mine & jnp.logical_not(home))
    def _():
        pltpu.make_async_copy(own_far, far, sem).start()
        pltpu.make_async_copy(own_near, near, sem).start()

    @pl.when(jnp.logical_not(mine))
    def _():
        pltpu.make_async_copy(other_far, far, sem).start()
        pltpu.make_async_copy(other_near, near, sem).start()


def load_wait(sources, target, sem):
    pltpu.make_async_copy(sources[0], target, sem).wait()


def put_pieces(total, first, second, others):
    rows = first.shape[0]
    first[...] = total[:rows].astype(BF16)
    second[...] = total[rows : 2 * rows].astype(BF16)
    others[...] = total[2 * rows :].astype(BF16)


def joined(pieces):
    return jnp.concatenate([piece[...] for piece in pieces], axis=0)


def head_scale2(values, masks):
    squares = values * values
    first = jnp.sum(jnp.where(masks[0], squares, 0.0), axis=-1, keepdims=True)
    second = jnp.sum(jnp.where(masks[0], 0.0, squares), axis=-1, keepdims=True)
    return jnp.where(
        masks[0],
        lax.rsqrt(first / HDIM + head_epsilon),
        lax.rsqrt(second / HDIM + head_epsilon),
    )


def head_mean2(values, masks):
    first = jnp.sum(jnp.where(masks[0], values, 0.0), axis=-1, keepdims=True)
    second = jnp.sum(jnp.where(masks[0], 0.0, values), axis=-1, keepdims=True)
    return jnp.where(masks[0], first, second) / HDIM


def norm_kernel(x, gain, normed):
    values = x[...].astype(F32)
    scale = lax.rsqrt(jnp.mean(values * values, axis=-1, keepdims=True) + epsilon)
    normed[...] = (values * scale * gain[...]).astype(BF16)


def summed(own, across, far):
    rows = own.shape[0]
    return own[...].astype(F32) + across[:rows, :].astype(F32) + far[...].astype(F32)


def branch_kernel(x, own, across, far, gain, total, normed):
    values = x[...].astype(F32) + summed(own, across, far)
    kept = values.astype(total.dtype)
    total[...] = kept
    values = kept.astype(F32)
    scale = lax.rsqrt(jnp.mean(values * values, axis=-1, keepdims=True) + epsilon)
    normed[...] = (values * scale * gain[...]).astype(BF16)


def end_kernel(x, own, across, far, total):
    total[...] = (x[...].astype(F32) + summed(own, across, far)).astype(total.dtype)


def back_kernel(x, own, across, far, residual, gain, wide, narrow, grad_gain):
    values = x[...].astype(F32)
    grad_normed = summed(own, across, far)
    scale = lax.rsqrt(jnp.mean(values * values, axis=-1, keepdims=True) + epsilon)
    unit = values * scale
    grad_unit = grad_normed * gain[...]
    centre = jnp.mean(grad_unit * unit, axis=-1, keepdims=True)
    total = scale * (grad_unit - unit * centre) + residual[...].astype(F32)
    wide[...] = total
    narrow[...] = total.astype(BF16)
    grad_gain[...] = jnp.sum(grad_normed * unit, axis=0, keepdims=True)


def diag_probs(query, keys, masks, allowed):
    scores = nt(stack2(query, masks), keys) * HDIM ** (-0.5)
    scores = jnp.where(allowed, scores, far_below)
    powers = jnp.exp(scores - jnp.max(scores, axis=-1, keepdims=True))
    return powers * (1.0 / jnp.sum(powers, axis=-1, keepdims=True))


def diag_allowed(columns, rows_meta, heads, rows):
    at, before, _ = stacked_position(rows)
    near = (at >= before) & ((at // BLOCK) == (before // BLOCK))
    return near & same_segment(columns, rows_meta, heads)


def diag_forward_kernel(layer, heads, *refs):
    flags, a0, a1, a2, a3, columns, rows_meta = refs[:7]
    qkv_from, out_from = refs[7:12], refs[12:17]
    chosen, mixed, first, second, others, w_qkv, w_out, sems = refs[17:]
    load_start(flags, layer, qkv_from, w_qkv, sems.at[0])
    load_start(flags, layer, out_from, w_out, sems.at[1])
    x = joined((a0, a1, a2, a3))
    rows = a0.shape[0]
    width = heads * HDIM
    depth = x.shape[1]
    masks = lane_masks(rows)
    load_wait(qkv_from, w_qkv, sems.at[0])
    for part in range(3):
        product = nn(x, w_qkv[part * depth : (part + 1) * depth, :])
        chosen[:, part * width : (part + 1) * width] = product.astype(BF16)
    for piece in range(4):
        span = slice(piece * rows, (piece + 1) * rows)
        allowed = diag_allowed(columns[span, :], rows_meta[piece], heads, rows)
        for pair in range(heads // 2):
            q, k, v = (
                chosen[span, part * width + pair * PAIR : part * width + (pair + 1) * PAIR]
                for part in range(3)
            )
            weights = diag_probs(q, k, masks, allowed).astype(BF16)
            mixed[span, pair * PAIR : (pair + 1) * PAIR] = pick(nn(weights, v), masks).astype(BF16)
    load_wait(out_from, w_out, sems.at[1])
    put_pieces(nn(mixed[...], w_out[...]), first, second, others)


def diag_backward_kernel(layer, heads, *refs):
    flags, a0, a1, a2, a3, chosen, columns, rows_meta = refs[:8]
    qkv_from, out_from = refs[8:13], refs[13:18]
    grads, first, second, others, w_qkv, w_out, sems = refs[18:]
    load_start(flags, layer, out_from, w_out, sems.at[1])
    load_start(flags, layer, qkv_from, w_qkv, sems.at[0])
    g = joined((a0, a1, a2, a3))
    rows = a0.shape[0]
    width = heads * HDIM
    depth = g.shape[1]
    masks = lane_masks(rows)
    load_wait(out_from, w_out, sems.at[1])
    grad_mixed = nt(g, w_out[...]).astype(BF16)
    for piece in range(4):
        span = slice(piece * rows, (piece + 1) * rows)
        allowed = diag_allowed(columns[span, :], rows_meta[piece], heads, rows)
        for pair in range(heads // 2):
            q, k, v = (
                chosen[span, part * width + pair * PAIR : part * width + (pair + 1) * PAIR]
                for part in range(3)
            )
            grad = stack2(grad_mixed[span, pair * PAIR : (pair + 1) * PAIR], masks)
            probs = diag_probs(q, k, masks, allowed)
            grad_probs = nt(grad, v)
            centre = jnp.sum(grad_probs * probs, axis=-1, keepdims=True)
            grad_scores = (probs * (grad_probs - centre)).astype(BF16)
            grad_q = pick(nn(grad_scores, k), masks) * HDIM ** (-0.5)
            grad_k = tn(grad_scores, stack2(q, masks)) * HDIM ** (-0.5)
            grad_v = tn(probs.astype(BF16), grad)
            for part, member in enumerate((grad_q, grad_k, grad_v)):
                at = part * width + pair * PAIR
                grads[span, at : at + PAIR] = member.astype(BF16)
    load_wait(qkv_from, w_qkv, sems.at[0])
    put_back(grads, w_qkv, width, depth, first, second, others)


def put_back(grads, w_qkv, width, depth, first, second, others):
    total = nt(grads[:, :width], w_qkv[:depth, :])
    for part in range(1, 3):
        total = total + nt(
            grads[:, part * width : (part + 1) * width],
            w_qkv[part * depth : (part + 1) * depth, :],
        )
    put_pieces(total, first, second, others)


def norm_project_kernel(layer, heads, *refs):
    flags, coefs, a0, a1, a2, a3, columns = refs[:7]
    qkv_from = refs[7:12]
    chosen, slopes, states, ranges, w_qkv, sems = refs[12:]
    load_start(flags, layer, qkv_from, w_qkv, sems.at[0])
    x = joined((a0, a1, a2, a3))
    rows = a0.shape[0]
    width = heads * HDIM
    depth = x.shape[1]
    masks = lane_masks(rows)
    load_wait(qkv_from, w_qkv, sems.at[0])
    for part in range(3):
        product = nn(x, w_qkv[part * depth : (part + 1) * depth, :])
        if part < 2:
            sigmoid = 1.0 / (1.0 + jnp.exp(-product))
            slope = sigmoid * (1.0 + product * (1.0 - sigmoid))
            slopes[:, part * width : (part + 1) * width] = slope.astype(BF16)
            product = product * sigmoid
        chosen[:, part * width : (part + 1) * width] = product.astype(BF16)
    mask = block_diagonal()
    pairs = heads // 2
    for half in range(2):
        whole = []
        for pair in range(pairs):
            total = jnp.zeros((PAIR, PAIR), F32)
            for piece in (2 * half, 2 * half + 1):
                span = slice(piece * rows, (piece + 1) * rows)
                at = width + pair * PAIR
                k = chosen[span, at : at + PAIR].astype(F32)
                v = chosen[span, at + width : at + width + PAIR]
                kept = spread2(columns[span, :], heads + 1 + heads + 2 * pair, masks)
                state = jnp.where(mask, tn((k * kept).astype(BF16), v), 0.0)
                base = (piece * pairs + pair) * PAIR
                states[base : base + PAIR, :] = state.astype(BF16)
                u = (2 * 4 + piece) * heads + 2 * pair
                total = total + by_rows(coefs[u], coefs[u + 1]) * state
            whole.append(total)
        ranges[half * PAIR : (half + 1) * PAIR, :] = pack_states(*whole).astype(BF16)


def norm_weight(columns, rows_meta, heads, pair, rows):
    at, before, top = stacked_position(rows)
    first, second = 2 * pair, 2 * pair + 1
    cumul = jnp.concatenate(
        [columns[:, first : first + 1], columns[:, second : second + 1]], axis=0
    )
    other = jnp.where(top, rows_meta[first : first + 1, :], rows_meta[second : second + 1, :])
    allowed = (at >= before) & same_segment(columns, rows_meta, heads)
    return jnp.where(allowed, jnp.exp(jnp.minimum(cumul - other, 0.0)), 0.0)


def norm_inner_kernel(heads, chosen, columns, rows_meta, inner):
    rows = rows_meta.shape[2]
    width = heads * HDIM
    masks = lane_masks(rows)
    for piece in range(4):
        span = slice(piece * rows, (piece + 1) * rows)
        for pair in range(heads // 2):
            q, k, v = (
                chosen[span, part * width + pair * PAIR : part * width + (pair + 1) * PAIR]
                for part in range(3)
            )
            weight = norm_weight(columns[span, :], rows_meta[piece], heads, pair, rows)
            scored = (nt(stack2(q, masks), k) * weight).astype(BF16)
            inner[span, pair * PAIR : (pair + 1) * PAIR] = pick(nn(scored, v), masks)


def norm_outer_kernel(layer, heads, *refs):
    flags, coefs, weights, chosen, inner, states, every, columns = refs[:8]
    out_from = refs[8:13]
    raw, mixed, entering, first, second, others, w_out, sems = refs[13:]
    load_start(flags, layer, out_from, w_out, sems.at[0])
    rows = first.shape[0]
    width = heads * HDIM
    masks = lane_masks(rows)
    pairs = heads // 2
    prefixes = [unpack_states(chain_sum(every, weights, half, heads)) for half in range(2)]
    for piece in range(4):
        span = slice(piece * rows, (piece + 1) * rows)
        for pair in range(pairs):
            a = piece * heads + 2 * pair
            b = (4 + piece) * heads + 2 * pair
            base = ((piece ^ 1) * pairs + pair) * PAIR
            state = by_rows(coefs[a], coefs[a + 1]) * prefixes[piece // 2][pair]
            state = state + by_rows(coefs[b], coefs[b + 1]) * states[base : base + PAIR, :].astype(
                F32
            )
            state = state.astype(BF16)
            base = (piece * pairs + pair) * PAIR
            entering[base : base + PAIR, :] = state
            lanes = slice(pair * PAIR, (pair + 1) * PAIR)
            reach = spread2(columns[span, :], heads + 1 + 2 * pair, masks)
            out = inner[span, lanes] + reach * nn(chosen[span, lanes], state)
            raw[span, lanes] = out
            mixed[span, lanes] = (out * head_scale2(out, masks)).astype(BF16)
    load_wait(out_from, w_out, sems.at[0])
    put_pieces(nn(mixed[...], w_out[...]), first, second, others)


def norm_back_raw_kernel(layer, heads, *refs):
    flags, coefs, a0, a1, a2, a3, raw, chosen, columns = refs[:9]
    out_from = refs[9:14]
    grad_raw, grad_states, ranges, w_out, sems = refs[14:]
    load_start(flags, layer, out_from, w_out, sems.at[0])
    g = joined((a0, a1, a2, a3))
    rows = a0.shape[0]
    masks = lane_masks(rows)
    mask = block_diagonal()
    pairs = heads // 2
    load_wait(out_from, w_out, sems.at[0])
    grad_mixed = nt(g, w_out[...])
    for half in range(2):
        whole = []
        for pair in range(pairs):
            total = jnp.zeros((PAIR, PAIR), F32)
            lanes = slice(pair * PAIR, (pair + 1) * PAIR)
            for piece in (2 * half, 2 * half + 1):
                span = slice(piece * rows, (piece + 1) * rows)
                out = raw[span, lanes]
                scale = head_scale2(out, masks)
                unit = out * scale
                grad = grad_mixed[span, lanes]
                grad = (scale * (grad - unit * head_mean2(grad * unit, masks))).astype(BF16)
                grad_raw[span, lanes] = grad
                reach = spread2(columns[span, :], heads + 1 + 2 * pair, masks)
                q = (chosen[span, lanes].astype(F32) * reach).astype(BF16)
                state = jnp.where(mask, tn(q, grad), 0.0)
                base = (piece * pairs + pair) * PAIR
                grad_states[base : base + PAIR, :] = state.astype(BF16)
                a = piece * heads + 2 * pair
                total = total + by_rows(coefs[a], coefs[a + 1]) * state
            whole.append(total)
        ranges[half * PAIR : (half + 1) * PAIR, :] = pack_states(*whole).astype(BF16)


def norm_back_inner_kernel(heads, grad_raw, chosen, entering, columns, rows_meta, grads):
    rows = rows_meta.shape[2]
    width = heads * HDIM
    masks = lane_masks(rows)
    pairs = heads // 2
    for piece in range(4):
        span = slice(piece * rows, (piece + 1) * rows)
        for pair in range(pairs):
            lanes = slice(pair * PAIR, (pair + 1) * PAIR)
            q, k, v = (
                chosen[span, part * width + pair * PAIR : part * width + (pair + 1) * PAIR]
                for part in range(3)
            )
            weight = norm_weight(columns[span, :], rows_meta[piece], heads, pair, rows)
            queries = stack2(q, masks)
            scored = (nt(queries, k) * weight).astype(BF16)
            grad = grad_raw[span, lanes]
            stacked = stack2(grad, masks)
            grad_dots = (nt(stacked, v) * weight).astype(BF16)
            base = (piece * pairs + pair) * PAIR
            reach = spread2(columns[span, :], heads + 1 + 2 * pair, masks)
            grad_q = pick(nn(grad_dots, k), masks)
            grad_q = grad_q + reach * nt(grad, entering[base : base + PAIR, :])
            for part, member in enumerate((grad_q, tn(grad_dots, queries), tn(scored, stacked))):
                at = part * width + pair * PAIR
                grads[span, at : at + PAIR] = member


def norm_back_outer_kernel(layer, heads, *refs):
    flags, coefs, weights, partial, chosen, slopes, grad_states, every, columns = refs[:9]
    qkv_from = refs[9:14]
    grads, first, second, others, w_qkv, sems = refs[14:]
    load_start(flags, layer, qkv_from, w_qkv, sems.at[0])
    rows = first.shape[0]
    depth = first.shape[1]
    width = heads * HDIM
    masks = lane_masks(rows)
    pairs = heads // 2
    suffixes = [unpack_states(chain_sum(every, weights, half, heads)) for half in range(2)]
    for piece in range(4):
        span = slice(piece * rows, (piece + 1) * rows)
        for pair in range(pairs):
            b = (4 + (piece ^ 1)) * heads + 2 * pair
            u = (8 + piece) * heads + 2 * pair
            base = ((piece ^ 1) * pairs + pair) * PAIR
            state = by_rows(coefs[u], coefs[u + 1]) * suffixes[piece // 2][pair]
            state = state + by_rows(coefs[b], coefs[b + 1]) * grad_states[
                base : base + PAIR, :
            ].astype(F32)
            state = state.astype(BF16)
            at = pair * PAIR
            kept = spread2(columns[span, :], heads + 1 + heads + 2 * pair, masks)
            k = chosen[span, width + at : width + at + PAIR].astype(F32) * kept
            v = chosen[span, 2 * width + at : 2 * width + at + PAIR]
            grad_q = partial[span, at : at + PAIR]
            grad_k = partial[span, width + at : width + at + PAIR] + kept * nt(v, state)
            grad_v = partial[span, 2 * width + at : 2 * width + at + PAIR]
            grad_v = grad_v + nn(k.astype(BF16), state)
            grad_q = grad_q * slopes[span, at : at + PAIR].astype(F32)
            grad_k = grad_k * slopes[span, width + at : width + at + PAIR].astype(F32)
            grads[span, at : at + PAIR] = grad_q.astype(BF16)
            grads[span, width + at : width + at + PAIR] = grad_k.astype(BF16)
            grads[span, 2 * width + at : 2 * width + at + PAIR] = grad_v.astype(BF16)
    load_wait(qkv_from, w_qkv, sems.at[0])
    put_back(grads, w_qkv, width, depth, first, second, others)


def mixer_weights_kernel(heads, x0, x1, x2, x3, g0, g1, g2, g3, grads, mixed, out):
    x = joined((x0, x1, x2, x3))
    g = joined((g0, g1, g2, g3))
    depth = x.shape[1]
    width = heads * HDIM
    for part in range(3):
        product = tn(x, grads[:, part * width : (part + 1) * width])
        out[part * depth : (part + 1) * depth, :] = product.astype(BF16)
    out[3 * depth :, :] = tn(g, mixed[...]).astype(BF16)


def glu_forward_kernel(layer, *refs):
    flags, a0, a1, a2, a3 = refs[:5]
    gate_from, down_from = refs[5:10], refs[10:15]
    gates, ups, hiddens, first, second, others, w_gate, w_down, sems = refs[15:]
    load_start(flags, layer, gate_from, w_gate, sems.at[0])
    load_start(flags, layer, down_from, w_down, sems.at[1])
    x = joined((a0, a1, a2, a3))
    extent = gates.shape[1]
    load_wait(gate_from, w_gate, sems.at[0])
    for at, size in tiles(extent):
        gate = nt(x, w_gate[at : at + size, :])
        up = nt(x, w_gate[extent + at : extent + at + size, :])
        gates[:, at : at + size] = gate.astype(BF16)
        ups[:, at : at + size] = up.astype(BF16)
        hiddens[:, at : at + size] = (gate * up).astype(BF16)
    load_wait(down_from, w_down, sems.at[1])
    rows = a0.shape[0]
    for at, size in tiles(x.shape[1]):
        total = nn(hiddens[...], w_down[:, at : at + size])
        put_tile(total, rows, at, size, first, second, others)


def put_tile(total, rows, at, size, first, second, others):
    first[:, at : at + size] = total[:rows].astype(BF16)
    second[:, at : at + size] = total[rows : 2 * rows].astype(BF16)
    others[:, at : at + size] = total[2 * rows :].astype(BF16)


def glu_backward_kernel(layer, *refs):
    flags, a0, a1, a2, a3, gates, ups = refs[:7]
    gate_from, down_from = refs[7:12], refs[12:17]
    grad_gates, grad_ups, first, second, others, w_gate, w_down, sems = refs[17:]
    load_start(flags, layer, down_from, w_down, sems.at[1])
    load_start(flags, layer, gate_from, w_gate, sems.at[0])
    g = joined((a0, a1, a2, a3))
    extent = gates.shape[1]
    load_wait(down_from, w_down, sems.at[1])
    for at, size in tiles(extent):
        grad = nt(g, w_down[at : at + size, :])
        grad_gates[:, at : at + size] = (grad * ups[:, at : at + size].astype(F32)).astype(BF16)
        grad_ups[:, at : at + size] = (grad * gates[:, at : at + size].astype(F32)).astype(BF16)
    load_wait(gate_from, w_gate, sems.at[0])
    rows = a0.shape[0]
    for at, size in tiles(g.shape[1]):
        total = nn(grad_gates[...], w_gate[:extent, at : at + size])
        total = total + nn(grad_ups[...], w_gate[extent:, at : at + size])
        put_tile(total, rows, at, size, first, second, others)


def glu_weights_kernel(x0, x1, x2, x3, g0, g1, g2, g3, grad_gates, grad_ups, hiddens, out):
    x = joined((x0, x1, x2, x3))
    g = joined((g0, g1, g2, g3))
    extent = hiddens.shape[1]
    for at, size in tiles(extent):
        out[at : at + size, :] = tn(grad_gates[:, at : at + size], x).astype(BF16)
        out[extent + at : extent + at + size, :] = tn(grad_ups[:, at : at + size], x).astype(BF16)
        out[2 * extent + at : 2 * extent + at + size, :] = tn(
            hiddens[:, at : at + size], g
        ).astype(BF16)


VM = pl.BlockSpec(memory_space=pltpu.VMEM)
SM = pl.BlockSpec(memory_space=pltpu.SMEM)
ANY = pl.BlockSpec(memory_space=pl.ANY)


def call(kernel, name, operands, outs, scratch=(), flops=0):
    specs = [spec for spec, _ in operands]
    values = [value for _, value in operands]
    moved = sum(v.size * v.dtype.itemsize for v in values) + sum(
        jnp.dtype(kind).itemsize * functools.reduce(lambda a, b: a * b, shape) for shape, kind in outs
    )
    result = pl.pallas_call(
        kernel,
        name=name,
        out_shape=[jax.ShapeDtypeStruct(shape, kind) for shape, kind in outs],
        in_specs=specs,
        out_specs=[VM] * len(outs),
        scratch_shapes=list(scratch),
        compiler_params=pltpu.CompilerParams(vmem_limit_bytes=vmem_limit),
        cost_estimate=pl.CostEstimate(flops=flops, bytes_accessed=moved, transcendentals=0),
    )(*values)
    return result


def vm(*values):
    return [(VM, value) for value in values]


def sm(*values):
    return [(SM, value) for value in values]


def hbm(*values):
    return [(ANY, value) for value in values]


class Place:
    def __init__(self):
        self.seqs = lax.axis_size("seq")
        self.tensors = lax.axis_size("tensor")
        self.section = lax.axis_index("section")
        self.seq = lax.axis_index("seq")
        self.tensor = lax.axis_index("tensor")
        self.core = self.seq % 2
        self.upper = (self.seq // 2) % 2
        self.inner = self.tensor % 2
        self.outer = self.tensor // 2
        self.home = self.core == self.outer

    def pairs(self, chosen, move):
        return [
            (s * self.tensors + t, move(s, t)[0] * self.tensors + move(s, t)[1])
            for s in range(self.seqs)
            for t in range(self.tensors)
            if chosen(s % 2 == t // 2)
        ]

    def joint(self, value, chosen, move):
        return lax.ppermute(value, ("seq", "tensor"), self.pairs(chosen, move))

    def over_seq(self, value, bit):
        return lax.ppermute(value, "seq", [(s, s ^ bit) for s in range(self.seqs)])

    def over_tensor(self, value, bit):
        return lax.ppermute(value, "tensor", [(t, t ^ bit) for t in range(self.tensors)])

    def over_section(self, value):
        return lax.ppermute(value, "section", [(0, 1), (1, 0)])


def half_of(array, which):
    half = array.shape[0] // 2
    return lax.dynamic_slice_in_dim(array, which * half, half, 0)


def fetch(place, own):
    part = half_of(own, place.upper)
    own_far = place.joint(part, lambda home: home, lambda s, t: (s, t ^ 2))
    part = jnp.where(place.home, part, own_far)
    other_far = place.over_section(part)
    own_near = place.joint(part, lambda home: not home, lambda s, t: (s ^ 2, t))
    other_near = place.over_seq(other_far, 2)
    return (own, own_far, own_near, other_far, other_near)


def gather_rows(place, own):
    far = place.over_tensor(own, 1)
    across = place.over_seq(own, 1)
    both = place.over_seq(far, 1)
    return (own, far, across, both)


def scatter_rows(place, first, second, others):
    across = place.over_seq(others, 1)
    rows = first.shape[0]
    sent = (second.astype(F32) + across[rows:].astype(F32)).astype(BF16)
    return (first, across, place.over_tensor(sent, 1))


def gather_states(place, own):
    every = jnp.concatenate([own, place.over_tensor(own, 2)], axis=0)
    bit = 2
    while bit < place.seqs:
        every = jnp.concatenate([every, place.over_seq(every, bit)], axis=0)
        bit *= 2
    return every


def reduce_grads(place, grads, layer):
    sent = half_of(grads, 1 - place.upper)
    total = half_of(grads, place.upper)

    def add(a, b):
        return (a.astype(F32) + b.astype(F32)).astype(BF16)

    total = add(total, place.over_seq(sent, 2))
    bit = 4
    while bit < place.seqs:
        total = add(total, place.over_seq(total, bit))
        bit *= 2
    total = add(total, lax.ppermute(total, "section", [(1 - layer, layer)]))
    total = add(total, place.joint(total, lambda home: not home, lambda s, t: (s, t ^ 2)))
    near = place.joint(total, lambda home: home, lambda s, t: (s ^ 2, t))
    total = jnp.where(
        place.home, total, place.joint(total, lambda home: home, lambda s, t: (s ^ 1, t))
    )
    near = jnp.where(
        place.home, near, place.joint(near, lambda home: home, lambda s, t: (s ^ 1, t))
    )
    low = jnp.where(place.upper == 0, total, near)
    high = jnp.where(place.upper == 0, near, total)
    return jnp.concatenate([low, high], axis=0)


def member_ids(place):
    ids = [(0, 0), (0, 1)]
    bit = 2
    while bit < place.seqs:
        ids = ids + [(s | bit, k) for s, k in ids]
        bit *= 2
    return ids


def prepare(place, log_decay, segments, rows):
    heads = log_decay.shape[0]
    seqs, tensors = place.seqs, place.tensors
    shard = place.inner + 2 * place.core
    seg_all = lax.all_gather(segments, "seq", axis=0).reshape(seqs * tensors, rows)
    lasts = seg_all[:, -1]
    before = jnp.concatenate([jnp.full((1,), -1.0, F32), lasts[:-1]])
    decay_all = lax.all_gather(log_decay, ("seq", "tensor"), axis=0)
    decay_all = decay_all.reshape(seqs, tensors, heads, tensors, rows)
    decay_all = lax.dynamic_index_in_dim(decay_all, shard, 1, keepdims=False)
    decay_all = jnp.transpose(decay_all, (0, 2, 1, 3)).reshape(seqs * tensors, heads, rows)
    pair_seq = place.seq - place.core
    seqs_of = [place.seq, place.seq, place.seq ^ 1, place.seq ^ 1]
    tensors_of = [place.tensor, place.tensor ^ 1, place.tensor, place.tensor ^ 1]
    ids = [s * tensors + t for s, t in zip(seqs_of, tensors_of)]
    decay = jnp.stack(
        [lax.dynamic_index_in_dim(decay_all, at, 0, keepdims=False) for at in ids]
    )
    seg = jnp.stack([lax.dynamic_index_in_dim(seg_all, at, 0, keepdims=False) for at in ids])
    prior = jnp.stack([lax.dynamic_index_in_dim(before, at, 0, keepdims=False) for at in ids])
    upto = (jnp.arange(rows)[:, None] <= jnp.arange(rows)[None, :]).astype(F32)
    cumul = jnp.einsum("phu,ut->pht", decay, upto, precision=lax.Precision.HIGHEST)
    total = cumul[:, :, -1]
    last = seg[:, -1]
    reach = jnp.exp(cumul) * (seg == prior[:, None])[:, None]
    kept = jnp.exp(total[:, :, None] - cumul) * (seg == last[:, None])[:, None]
    rows_meta = jnp.concatenate([cumul, seg[:, None]], axis=1)
    columns = jnp.concatenate([cumul, seg[:, None], reach, kept], axis=1)
    columns = jnp.transpose(columns, (0, 2, 1)).reshape(4 * rows, 3 * heads + 1)
    order = jnp.array([0, 1, 0, 1]) ^ place.inner
    second = (order == 1)[:, None]
    partner = jnp.array([1, 0, 3, 2])
    carried = jnp.exp(total) * (prior == last)[:, None]
    a = jnp.where(second, carried[partner], 1.0)
    b = jnp.where(second, jnp.ones_like(a), 0.0)
    u = jnp.where(second, 1.0, carried[partner])
    coefs = jnp.stack([a, b, u]).reshape(-1)
    piece_totals = jnp.sum(decay_all, axis=-1)
    range_totals = jnp.sum(piece_totals.reshape(-1, 2, heads), axis=1)
    range_lasts = lasts[1::2]
    range_prior = before[::2]
    count = range_totals.shape[0]
    included = jnp.cumsum(range_totals, axis=0)
    excluded = included - range_totals
    apart = excluded[:, None] - included[None, :]
    linked = (jnp.arange(count)[:, None] > jnp.arange(count)[None, :]) & (
        range_prior[:, None] == range_lasts[None, :]
    )
    matrix = jnp.where(linked[..., None], jnp.exp(jnp.minimum(apart, 0.0)), 0.0)
    members = jnp.array(member_ids(place))
    member_seq = members[:, 0] ^ (place.seq - place.core)
    member_outer = members[:, 1] ^ place.outer
    cores = jnp.stack([place.core, 1 - place.core])
    every = ((member_seq[:, None] + cores[None, :]) * 2 + member_outer[:, None]).reshape(-1)
    mine = (place.seq - place.core + cores) * 2 + place.outer
    pick_every = (every[:, None] == jnp.arange(count)[None, :]).astype(F32)
    pick_mine = (mine[:, None] == jnp.arange(count)[None, :]).astype(F32)
    exact = lax.Precision.HIGHEST
    forward = jnp.einsum("ar,rsh,js->ajh", pick_mine, matrix, pick_every, precision=exact)
    backward = jnp.einsum("as,rsh,jr->ajh", pick_mine, matrix, pick_every, precision=exact)
    return columns, rows_meta, coefs, forward.reshape(-1), backward.reshape(-1)


def body(tokens, w_qkv, w_out, w_gate_up, w_down, norm_gains, log_decay, segment_ids, cotangent):
    place = Place()
    section = place.section
    rows, depth = tokens.shape[1:]
    heads = w_qkv.shape[-1] // HDIM
    width = heads * HDIM
    extent = w_gate_up.shape[-1]
    count = 4 * rows
    flags = jnp.stack([section, place.upper, place.home.astype(jnp.int32)]).astype(jnp.int32)

    def one_stream(array):
        return lax.dynamic_index_in_dim(array, section, 0, keepdims=False)

    x0 = one_stream(tokens)
    out_cotangent = one_stream(cotangent)
    gains_own = norm_gains[0]
    gains_other = place.over_section(gains_own)
    gains = [
        jnp.where(section == layer, gains_own, gains_other)[:, None, :] for layer in range(2)
    ]

    row_bf = ((rows, depth), BF16)
    row_f32 = ((rows, depth), F32)
    pieces = [row_bf, row_bf, ((2 * rows, depth), BF16)]
    dma = pltpu.SemaphoreType.DMA((2,))

    def normalise(x, gain):
        return call(norm_kernel, "normalise", vm(x, gain), [row_bf])[0]

    qkv_from = fetch(place, jnp.transpose(w_qkv[0], (1, 0, 2)).reshape(3 * depth, width))
    out_from = fetch(place, w_out[0])
    gate_from = fetch(
        place, jnp.transpose(w_gate_up[0], (1, 2, 0)).reshape(2 * extent, depth)
    )
    down_from = fetch(place, w_down[0])
    s_qkv = pltpu.VMEM((3 * depth, width), BF16)
    s_out = pltpu.VMEM((width, depth), BF16)
    s_gate = pltpu.VMEM((2 * extent, depth), BF16)
    s_down = pltpu.VMEM((extent, depth), BF16)

    columns, rows_meta, coefs, forward_weights, backward_weights = prepare(
        place,
        jnp.transpose(one_stream(log_decay), (1, 0)),
        one_stream(segment_ids).astype(F32),
        rows,
    )

    def branch(x, parts, gain, kind):
        return call(
            branch_kernel, "branch", vm(x, *parts, gain), [((rows, depth), kind), row_bf]
        )

    def glu_forward(layer, gathered):
        *kept, p0, p1, p2 = call(
            functools.partial(glu_forward_kernel, layer),
            "glu_forward",
            sm(flags) + vm(*gathered) + hbm(*gate_from, *down_from),
            [((count, extent), BF16)] * 3 + pieces,
            [s_gate, s_down, dma],
            6 * count * extent * depth,
        )
        return kept, scatter_rows(place, p0, p1, p2)

    def glu_backward(layer, gathered, kept):
        gates, ups, hiddens = kept
        grad_gates, grad_ups, p0, p1, p2 = call(
            functools.partial(glu_backward_kernel, layer),
            "glu_backward",
            sm(flags) + vm(*gathered, gates, ups) + hbm(*gate_from, *down_from),
            [((count, extent), BF16)] * 2 + pieces,
            [s_gate, s_down, dma],
            6 * count * extent * depth,
        )
        return (grad_gates, grad_ups, hiddens), scatter_rows(place, p0, p1, p2)

    def glu_weights(x, g, kept):
        return call(
            glu_weights_kernel,
            "glu_weights",
            vm(*x, *g, *kept),
            [((3 * extent, depth), BF16)],
            (),
            6 * count * extent * depth,
        )[0]

    def mixer_weights(x, g, grads, mixed):
        return call(
            functools.partial(mixer_weights_kernel, heads),
            "mixer_weights",
            vm(*x, *g, grads, mixed),
            [((4 * depth, width), BF16)],
            (),
            8 * count * width * depth,
        )[0]

    def back(x, parts, residual, gain):
        return call(
            back_kernel,
            "back",
            vm(x, *parts, residual, gain),
            [row_f32, row_bf, ((1, depth), F32)],
        )

    normed0 = gather_rows(place, normalise(x0, gains[0][0]))
    chosen0, mixed0, p0, p1, p2 = call(
        functools.partial(diag_forward_kernel, 0, heads),
        "diag_forward",
        sm(flags) + vm(*normed0, columns, rows_meta) + hbm(*qkv_from, *out_from),
        [((count, 3 * width), BF16), ((count, width), BF16)] + pieces,
        [s_qkv, s_out, dma],
        8 * count * width * depth,
    )
    middle0, hidden_in = branch(x0, scatter_rows(place, p0, p1, p2), gains[0][1], F32)
    hidden_in0 = gather_rows(place, hidden_in)
    kept0, parts = glu_forward(0, hidden_in0)
    x1, normed = branch(middle0, parts, gains[1][0], BF16)

    normed1 = gather_rows(place, normed)
    state_rows = 4 * (heads // 2) * PAIR
    chosen1, slopes, states, ranges = call(
        functools.partial(norm_project_kernel, 1, heads),
        "norm_project",
        sm(flags, coefs) + vm(*normed1, columns) + hbm(*qkv_from),
        [
            ((count, 3 * width), BF16),
            ((count, 2 * width), BF16),
            ((state_rows, PAIR), BF16),
            ((2 * PAIR, PAIR), BF16),
        ],
        [s_qkv, dma],
        6 * count * width * depth,
    )
    every = gather_states(place, ranges)
    (inner,) = call(
        functools.partial(norm_inner_kernel, heads),
        "norm_inner",
        vm(chosen1, columns, rows_meta),
        [((count, width), F32)],
        (),
        8 * count * width * rows,
    )
    raw, mixed1, entering, p0, p1, p2 = call(
        functools.partial(norm_outer_kernel, 1, heads),
        "norm_outer",
        sm(flags, coefs, forward_weights)
        + vm(chosen1, inner, states, every, columns)
        + hbm(*out_from),
        [((count, width), F32), ((count, width), BF16), ((state_rows, PAIR), BF16)] + pieces,
        [s_out, dma],
        2 * count * width * depth,
    )
    middle1, hidden_in = branch(x1, scatter_rows(place, p0, p1, p2), gains[1][1], F32)
    hidden_in1 = gather_rows(place, hidden_in)
    kept1, parts = glu_forward(1, hidden_in1)
    (y1,) = call(end_kernel, "layer_end", vm(middle1, *parts), [row_bf])

    grad_branch1 = gather_rows(place, out_cotangent)
    kept1, parts = glu_backward(1, grad_branch1, kept1)
    glu_grads1 = glu_weights(hidden_in1, grad_branch1, kept1)
    grad_middle, grad_narrow, gain_11 = back(middle1, parts, out_cotangent, gains[1][1])
    grad_attn1 = gather_rows(place, grad_narrow)
    grad_raw, grad_states, ranges = call(
        functools.partial(norm_back_raw_kernel, 1, heads),
        "norm_back_raw",
        sm(flags, coefs) + vm(*grad_attn1, raw, chosen1, columns) + hbm(*out_from),
        [((count, width), BF16), ((state_rows, PAIR), BF16), ((2 * PAIR, PAIR), BF16)],
        [s_out, dma],
        2 * count * width * depth,
    )
    every = gather_states(place, ranges)
    (partial,) = call(
        functools.partial(norm_back_inner_kernel, heads),
        "norm_back_inner",
        vm(grad_raw, chosen1, entering, columns, rows_meta),
        [((count, 3 * width), F32)],
        (),
        20 * count * width * rows,
    )
    grads1, p0, p1, p2 = call(
        functools.partial(norm_back_outer_kernel, 1, heads),
        "norm_back_outer",
        sm(flags, coefs, backward_weights)
        + vm(partial, chosen1, slopes, grad_states, every, columns)
        + hbm(*qkv_from),
        [((count, 3 * width), BF16)] + pieces,
        [s_qkv, dma],
        6 * count * width * depth,
    )
    parts = scatter_rows(place, p0, p1, p2)
    mixer_grads1 = mixer_weights(normed1, grad_attn1, grads1, mixed1)
    _, passed_grad, gain_10 = back(x1, parts, grad_middle, gains[1][0])

    grad_branch0 = gather_rows(place, passed_grad)
    kept0, parts = glu_backward(0, grad_branch0, kept0)
    glu_grads0 = glu_weights(hidden_in0, grad_branch0, kept0)
    grad_middle, grad_narrow, gain_01 = back(middle0, parts, passed_grad, gains[0][1])
    grad_attn0 = gather_rows(place, grad_narrow)
    grads0, p0, p1, p2 = call(
        functools.partial(diag_backward_kernel, 0, heads),
        "diag_backward",
        sm(flags) + vm(*grad_attn0, chosen0, columns, rows_meta) + hbm(*qkv_from, *out_from),
        [((count, 3 * width), BF16)] + pieces,
        [s_qkv, s_out, dma],
        8 * count * width * depth,
    )
    parts = scatter_rows(place, p0, p1, p2)
    mixer_grads0 = mixer_weights(normed0, grad_attn0, grads0, mixed0)
    first_grad, first_narrow, gain_00 = back(x0, parts, grad_middle, gains[0][0])

    glu_total = [reduce_grads(place, glu_grads0, 0), reduce_grads(place, glu_grads1, 1)]
    mixer_total = [reduce_grads(place, mixer_grads0, 0), reduce_grads(place, mixer_grads1, 1)]
    first = section == 0
    glu_total = jnp.where(first, *glu_total).astype(F32)
    mixer_total = jnp.where(first, *mixer_total).astype(F32)
    total_qkv = jnp.transpose(mixer_total[: 3 * depth].reshape(3, depth, width), (1, 0, 2))
    total_out = jnp.transpose(mixer_total[3 * depth :], (1, 0))
    total_gate_up = jnp.transpose(glu_total[: 2 * extent].reshape(2, extent, depth), (2, 0, 1))
    total_down = glu_total[2 * extent :]
    gains_all = jnp.concatenate([gain_00, gain_01, gain_10, gain_11], axis=0)
    gains_all = lax.psum(gains_all, ("section", "seq", "tensor"))
    total_gains = jnp.where(first, gains_all[:2], gains_all[2:])

    def both_streams(of_first, of_second, kind):
        kept = jnp.where(first, of_first, of_second)
        sent = jnp.where(first, of_second, of_first).astype(BF16)
        got = place.over_section(sent).astype(kind)
        kept = kept.astype(kind)
        return jnp.stack([jnp.where(first, kept, got), jnp.where(first, got, kept)])

    layer_outs = both_streams(x1, y1, BF16)
    input_grads = both_streams(first_grad, passed_grad.astype(F32), F32)
    return (
        layer_outs[None],
        input_grads[None],
        total_qkv[None],
        total_out[None],
        total_gate_up[None],
        total_down[None],
        total_gains[None],
    )


def solution(mesh):
    return jax.shard_map(
        body,
        mesh=mesh,
        in_specs=(
            P(None, ("seq", "tensor"), None),
            P("section", None, None, "tensor"),
            P("section", "tensor", None),
            P("section", None, None, "tensor"),
            P("section", "tensor", None),
            P("section", None, None),
            P(None, "seq", "tensor"),
            P(None, "seq"),
            P(None, ("seq", "tensor"), None),
        ),
        out_specs=(
            P("section", None, ("seq", "tensor"), None),
            P("section", None, ("seq", "tensor"), None),
            P("section", None, None, "tensor"),
            P("section", "tensor", None),
            P("section", None, None, "tensor"),
            P("section", "tensor", None),
            P("section", None, None),
        ),
        check_vma=False,
    )
```

time: 1670 us -> 836 us (0.50)
  local copies, waits for them, and re-layouts: 454 us -> 48.1 us
  other arithmetic: 392 us -> 69 us
  matrix products: 218 us -> 1.84 us
  starting transfers between devices: 12.7 us -> 173 us
  waiting for transfers between devices: 416 us -> 277 us
  Pallas kernels: 0 us -> 116 us
  blocking collectives: 101 us -> 140 us
  between operations: 27.6 us -> 2.42 us
  loops' own time: 24.2 us -> 0 us
    ppermute x4 -> x87, waiting for transfers between devices: 23.9 us -> 277 us  [the longest x34 84.8 us: over_seq(): return lax.ppermute(value, 'seq', [(s, s ^ bit) for s in range(self.seqs)])]
    dot_general x102 -> x5, matrix products: 218 us -> 1.84 us  [the longest x1 0.85 us: prepare(): jnp.einsum('phu,ut->pht', decay, upto, precision=lax.Precision.HIGHEST)]
    reduce_scatter x12 -> x0, waiting for transfers between devices: 169 us -> none  [the longest x6 133 us: scatter_rows(): lax.psum_scatter(partial_sum.astype(jnp.bfloat16), 'tensor', scatter_dime...]
    ppermute x4 -> x87, starting transfers between devices: 9.32 us -> 173 us  [the longest x34 72.3 us: over_seq(): return lax.ppermute(value, 'seq', [(s, s ^ bit) for s in range(self.seqs)])]
    all_gather x12 -> x0, waiting for transfers between devices: 135 us -> none  [the longest x6 88.1 us: gather_rows(): return lax.all_gather(shard_piece, 'tensor', axis=0, tiled=True)]
    pallas_call x0 -> x25, Pallas kernels: none -> 116 us  [call(): pl.pallas_call(kernel, name=name, out_shape=[jax.ShapeDtypeStruct(shape,...]
    add x72 -> x4, other arithmetic: 112 us -> 0.15 us  [the longest x1 0.08 us: prepare(): mine = (place.seq - place.core + cores) * 2 + place.outer]
    dynamic_update_slice x102 -> x0, other arithmetic: 92.8 us -> none  [the longest x72 47.9 us: norm_local(): lax.scan(advance, jnp.zeros(block_states.shape[1:], jnp.float32), (intern...]
  transfers between devices with their start and end apart: 29 -> 87, of which waited for: 21 -> 28; matrix products, arithmetic and copies ran while one was open for 30% -> 11% of each run, Pallas kernels for 0% -> 9%
where the time goes in v1:
time: 836 us; the launch traced here: 828 us
  waiting for transfers between devices  277 us (33%)
  starting transfers between devices  173 us (21%)
  blocking collectives  140 us (17%)
  Pallas kernels  116 us (14%)
  other arithmetic  69 us (8%)
  local copies, waits for them, and re-layouts  48.1 us (6%)
    pallas_call x25, Pallas kernels, call(): pl.pallas_call(kernel, name=name, out_shape=[jax.ShapeDtypeStruct(shape,...  116 us
    ppermute x34, waiting for transfers between devices, over_seq(): return lax.ppermute(value, 'seq', [(s, s ^ bit) for s in range(self.seqs)])  84.8 us
    psum x1, blocking collectives, body(): gains_all = lax.psum(gains_all, ('section', 'seq', 'tensor'))  79.2 us
    ppermute x18, waiting for transfers between devices, over_tensor(): lax.ppermute(value, 'tensor', [(t, t ^ bit) for t in range(self.tensors)])  74.8 us
    ppermute x34, starting transfers between devices, over_seq(): return lax.ppermute(value, 'seq', [(s, s ^ bit) for s in range(self.seqs)])  72.3 us
    ppermute x24, starting transfers between devices, joint(): return lax.ppermute(value, ('seq', 'tensor'), self.pairs(chosen, move))  57.3 us
    all_gather x1, blocking collectives, prepare(): decay_all = lax.all_gather(log_decay, ('seq', 'tensor'), axis=0)  56 us
    ppermute x24, waiting for transfers between devices, joint(): return lax.ppermute(value, ('seq', 'tensor'), self.pairs(chosen, move))  55.1 us
  transfers between devices with their start and end apart: 87, of which 28 were waited for; matrix products, arithmetic and copies ran while one was open for 11% of the time, Pallas kernels for 9%

profile of v1, /device:TPU:0, one launch (start us, length us, event | category | flops | bytes accessed | tf_op | source)
XLA Modules:
  0.0 828.3 jit_solution(6462044673089930684)
XLA Ops:
  0.7 3.0 collective-permute-start
  5.7 5.4 collective-permute-start.4
  19.9 5.2 all-gather.2
  32.8 56.0 %all-gather.1 = f32[16,4,512]{2,1,0:T(4,128)S(1)} all-gather(f32[1,4,512]{2,1,0:T(4,128)S(1)} %dynamic-slice_bitcast_fusion.5), channel_id=2, replica_groups=mesh['section'=2,'seq'=4,'tensor'=4] {'seq','tensor'}, dimensions={0}, use_global_device_ids=true | all-gather | bytes 139264 | tf_op jit(solution)/shard_map/all_gather | solution.py:727
  104.8 4.7 collective-permute-start.19
  117.2 5.4 collective-permute-start.21
  130.7 10.4 %collective-permute-done.11.refs_16_.refs_12_.refs_13_.refs_17_ = bf16[128,1024]{1,0:T(8,128)(2,1)} collective-permute-done((bf16[128,1024]{1,0:T(8,128)(2,1)S(1)}, bf16[128,1024]{1,0:T(8,128)(2,1)}, u32[]{:S(2)}, u32[]{:S(2)}) %collective-permute-start.11) | collective-permute-done | bytes 262176 | tf_op jit(solution)/shard_map/ppermute | solution.py:638
  142.3 7.8 diag_forward.1
  150.1 7.1 collective-permute-start.12
  164.9 11.6 %collective-permute-done.23.refs_13_.refs_15_ = bf16[352,1024]{1,0:T(8,128)(2,1)} collective-permute-done((bf16[352,1024]{1,0:T(8,128)(2,1)S(1)}, bf16[352,1024]{1,0:T(8,128)(2,1)}, u32[]{:S(2)}, u32[]{:S(2)}) %collective-permute-start.23) | collective-permute-done | bytes 720928 | tf_op jit(solution)/shard_map/ppermute | solution.py:644
  182.7 42.5 %collective-permute-start.15 = (bf16[128,1024]{1,0:T(8,128)(2,1)}, bf16[128,1024]{1,0:T(8,128)(2,1)S(1)}, u32[]{:S(2)}, u32[]{:S(2)}) collective-permute-start(bf16[128,1024]{1,0:T(8,128)(2,1)} %get-tuple-element.75.refs_1_.x0), channel_id=1, source_target_pairs={{0,4},{4,0},{8,12},{12,8},{1,5},{5,1},{9,13},{13,9},{2,6},{6,2},{1... | collective-permute-start | bytes 786440 | tf_op jit(solution)/shard_map/ppermute | solution.py:638
  227.3 6.7 glu_forward.2
  234.1 6.9 collective-permute-start.25
  246.2 6.3 collective-permute-done.26.far
  257.7 5.9 collective-permute-done.27.refs_3_.x1
  265.8 4.9 norm_project.1
  271.7 6.1 collective-permute-done.30
  281.2 2.9 norm_inner.1.refs_4_
  285.7 4.8 norm_outer.1
  294.2 8.1 collective-permute-done.33.far
  307.5 7.3 collective-permute-done.34.refs_2_.x1
  315.3 3.4 collective-permute-done.40.refs_2_.g1
  320.1 6.7 glu_forward.3
  327.7 6.8 glu_backward.2
  338.4 8.3 collective-permute-done.44.far
  347.3 2.7 back.4
  350.3 7.7 collective-permute-done.45.refs_3_.g1
  360.3 5.5 norm_back_raw.1
  367.1 5.1 collective-permute-done.48
  375.2 4.9 norm_back_inner.1.refs_3_
  380.8 5.3 norm_back_outer.1
  386.7 6.8 glu_weights.3
  396.5 5.4 collective-permute-done.51.far
  402.7 2.7 back.5
  405.6 7.5 collective-permute-done.52.refs_2_.g1
  414.7 4.4 mixer_weights.3
  419.9 6.8 glu_backward.3
  427.0 6.7 glu_weights.2
  433.7 3.3 constant_dynamic-slice_fusion
  444.5 3.7 collective-permute-done.56.far
  453.0 3.3 add_convert_fusion.2
  456.3 4.1 collective-permute-start.82
  461.0 52.6 %collective-permute-done.69 = bf16[2048,256]{1,0:T(8,128)(2,1)} collective-permute-done((bf16[2048,256]{1,0:T(8,128)(2,1)}, bf16[2048,256]{1,0:T(8,128)(2,1)}, u32[]{:S(2)}, u32[]{:S(2)}) %collective-permute-start.69) | collective-permute-done | bytes 1048608 | tf_op jit(solution)/shard_map/ppermute | solution.py:638
  515.3 3.6 collective-permute-start.70
  519.6 9.0 %diag_backward.1 = (bf16[512,768]{1,0:T(8,128)(2,1)}, bf16[128,1024]{1,0:T(8,128)(2,1)}, bf16[128,1024]{1,0:T(8,128)(2,1)}, bf16[256,1024]{1,0:T(8,128)(2,1)}) custom-call(s32[3]{0:T(128)} %pad_add_fusion.refs_0_, bf16[128,1024]{1,0:T(8,128)(2,1)} %get-tuple-element.114.refs_1_.g0, bf16[128,1024]{1,0:T(8,128)(2,1)} %copy-done.45, ...), custom_call_target="tpu_custom_call" | custom-call | flops 1073741824 | bytes 9998348 | tf_op jit(solution)/shard_map/diag_backward/pallas_call | solution.py:588
  528.7 4.4 mixer_weights.2
  540.4 2.8 collective-permute-start.39
  546.0 12.6 %collective-permute-done.63 = bf16[2048,256]{1,0:T(8,128)(2,1)S(1)} collective-permute-done((bf16[2048,256]{1,0:T(8,128)(2,1)S(1)}, bf16[2048,256]{1,0:T(8,128)(2,1)S(1)}, u32[]{:S(2)}, u32[]{:S(2)}) %collective-permute-start.63) | collective-permute-done | bytes 1048608 | tf_op jit(solution)/shard_map/ppermute | solution.py:638
  564.3 25.9 %collective-permute-done.76 = bf16[1056,1024]{1,0:T(8,128)(2,1)S(1)} collective-permute-done((bf16[1056,1024]{1,0:T(8,128)(2,1)S(1)}, bf16[1056,1024]{1,0:T(8,128)(2,1)S(1)}, u32[]{:S(2)}, u32[]{:S(2)}) %collective-permute-start.76) | collective-permute-done | bytes 2162720 | tf_op jit(solution)/shard_map/ppermute | solution.py:697
  592.8 23.1 %collective-permute-done.64 = bf16[2048,256]{1,0:T(8,128)(2,1)S(1)} collective-permute-done((bf16[2048,256]{1,0:T(8,128)(2,1)S(1)}, bf16[2048,256]{1,0:T(8,128)(2,1)S(1)}, u32[]{:S(2)}, u32[]{:S(2)}) %collective-permute-start.64) | collective-permute-done | bytes 1048608 | tf_op jit(solution)/shard_map/ppermute | solution.py:697
  621.1 4.7 collective-permute-start.72
  625.9 2.7 back.7
  630.0 3.6 collective-permute-start.73
  636.2 55.0 %collective-permute-done.65 = bf16[2048,256]{1,0:T(8,128)(2,1)} collective-permute-done((bf16[2048,256]{1,0:T(8,128)(2,1)}, bf16[2048,256]{1,0:T(8,128)(2,1)}, u32[]{:S(2)}, u32[]{:S(2)}) %collective-permute-start.65) | collective-permute-done | bytes 1048608 | tf_op jit(solution)/shard_map/ppermute | solution.py:635
  691.2 2.8 add_convert_fusion.9
  694.0 2.9 collective-permute-start.85
  696.9 2.9 collective-permute-start.67
  699.9 3.9 add_convert_fusion.3
  703.8 3.0 collective-permute-start.79
  711.1 79.2 %psum.7 = f32[4,1024]{1,0:T(4,128)S(1)} all-reduce(f32[4,1024]{1,0:T(4,128)S(1)} %pad_maximum_fusion.5), channel_id=1, replica_groups=mesh['section'=2,'seq'=4,'tensor'=4] {'section','seq','tensor'}, use_global_device_ids=true, to_apply=%region_3.4 | all-reduce | flops 4096 | bytes 32768 | tf_op jit(solution)/shard_map/psum | solution.py:1002
  794.6 2.7 collective-permute-start.84
  802.8 2.8 collective-permute-start.78
  818.0 2.7 broadcast_select_fusion.7
  823.0 3.0 slice.136
  (424 shorter events, 189.9 us)
Async XLA Ops:
  0.7 89.7 %collective-permute-start = (f32[2,1024]{1,0:T(2,128)}, f32[2,1024]{1,0:T(2,128)}, u32[]{:S(2)}, u32[]{:S(2)}) collective-permute-start(f32[2,1024]{1,0:T(2,128)} %bitcast.152), channel_id=1, source_target_pairs={{0,16},{16,0},{1,17},{17,1},{2,18},{18,2},{3,19},{19,3},{4,20},{20... | collective-permute-start | bytes 24584 | tf_op jit(solution)/shard_map/ppermute | solution.py:644
  5.7 86.0 %collective-permute-start.4 = (bf16[1536,256]{1,0:T(8,128)(2,1)}, bf16[1536,256]{1,0:T(8,128)(2,1)}, u32[]{:S(2)}, u32[]{:S(2)}) collective-permute-start(bf16[1536,256]{1,0:T(8,128)(2,1)} %constant_dynamic-slice_fusion.5), channel_id=1, source_target_pairs={{0,2},{1,3},{6,4},{7,5},{8,10},{9,11},{14,12},{15,13},{16,18},{17,... | collective-permute-start | bytes 2359304 | tf_op jit(solution)/shard_map/ppermute | solution.py:635
  12.8 86.4 %collective-permute-start.8 = (bf16[128,1024]{1,0:T(8,128)(2,1)}, bf16[128,1024]{1,0:T(8,128)(2,1)}, u32[]{:S(2)}, u32[]{:S(2)}) collective-permute-start(bf16[128,1024]{1,0:T(8,128)(2,1)} %dynamic-slice_bitcast_fusion.2), channel_id=1, source_target_pairs={{0,2},{1,3},{6,4},{7,5},{8,10},{9,11},{14,12},{15,13},{16,18},{17,... | collective-permute-start | bytes 786440 | tf_op jit(solution)/shard_map/ppermute | solution.py:635
  17.5 84.0 %collective-permute-start.17 = (bf16[704,1024]{1,0:T(8,128)(2,1)}, bf16[704,1024]{1,0:T(8,128)(2,1)}, u32[]{:S(2)}, u32[]{:S(2)}) collective-permute-start(bf16[704,1024]{1,0:T(8,128)(2,1)} %constant_dynamic-slice_fusion.4), channel_id=1, source_target_pairs={{0,2},{1,3},{6,4},{7,5},{8,10},{9,11},{14,12},{15,13},{16,18},{17,... | collective-permute-start | bytes 4325384 | tf_op jit(solution)/shard_map/ppermute | solution.py:635
  93.9 20.8 %collective-permute-start.6 = (bf16[1536,256]{1,0:T(8,128)(2,1)}, bf16[1536,256]{1,0:T(8,128)(2,1)}, u32[]{:S(2)}, u32[]{:S(2)}) collective-permute-start(bf16[1536,256]{1,0:T(8,128)(2,1)} %broadcast_select_fusion.17), channel_id=1, source_target_pairs={{0,16},{16,0},{1,17},{17,1},{2,18},{18,2},{3,19},{19,3},{4,20},{20... | collective-permute-start | bytes 2359304 | tf_op jit(solution)/shard_map/ppermute | solution.py:644
  99.1 13.0 %collective-permute-start.2 = (bf16[128,1024]{1,0:T(8,128)(2,1)}, bf16[128,1024]{1,0:T(8,128)(2,1)}, u32[]{:S(2)}, u32[]{:S(2)}) collective-permute-start(bf16[128,1024]{1,0:T(8,128)(2,1)} %normalise.1.refs_1_.x0), channel_id=1, source_target_pairs={{0,4},{4,0},{8,12},{12,8},{1,5},{5,1},{9,13},{13,9},{2,6},{6,2},{1... | collective-permute-start | bytes 786440 | tf_op jit(solution)/shard_map/ppermute | solution.py:638
  100.9 16.3 %collective-permute-start.9 = (bf16[128,1024]{1,0:T(8,128)(2,1)}, bf16[128,1024]{1,0:T(8,128)(2,1)S(1)}, u32[]{:S(2)}, u32[]{:S(2)}) collective-permute-start(bf16[128,1024]{1,0:T(8,128)(2,1)} %broadcast_select_fusion.19), channel_id=1, source_target_pairs={{2,10},{3,11},{4,12},{5,13},{10,2},{11,3},{12,4},{13,5},{18,26},{1... | collective-permute-start | bytes 786440 | tf_op jit(solution)/shard_map/ppermute | solution.py:635
  101.6 21.0 %collective-permute-start.10 = (bf16[128,1024]{1,0:T(8,128)(2,1)}, bf16[128,1024]{1,0:T(8,128)(2,1)S(1)}, u32[]{:S(2)}, u32[]{:S(2)}) collective-permute-start(bf16[128,1024]{1,0:T(8,128)(2,1)} %broadcast_select_fusion.19), channel_id=1, source_target_pairs={{0,16},{16,0},{1,17},{17,1},{2,18},{18,2},{3,19},{19,3},{4,20},{20... | collective-permute-start | bytes 786440 | tf_op jit(solution)/shard_map/ppermute | solution.py:644
  104.8 55.0 %collective-permute-start.19 = (bf16[704,1024]{1,0:T(8,128)(2,1)}, bf16[704,1024]{1,0:T(8,128)(2,1)S(1)}, u32[]{:S(2)}, u32[]{:S(2)}) collective-permute-start(bf16[704,1024]{1,0:T(8,128)(2,1)} %broadcast_select_fusion.8), channel_id=1, source_target_pairs={{0,16},{16,0},{1,17},{17,1},{2,18},{18,2},{3,19},{19,3},{4,20},{20... | collective-permute-start | bytes 4325384 | tf_op jit(solution)/shard_map/ppermute | solution.py:644
  112.1 29.0 %collective-permute-start.5 = (bf16[1536,256]{1,0:T(8,128)(2,1)}, bf16[1536,256]{1,0:T(8,128)(2,1)S(1)}, u32[]{:S(2)}, u32[]{:S(2)}) collective-permute-start(bf16[1536,256]{1,0:T(8,128)(2,1)} %broadcast_select_fusion.17), channel_id=1, source_target_pairs={{2,10},{3,11},{4,12},{5,13},{10,2},{11,3},{12,4},{13,5},{18,26},{1... | collective-permute-start | bytes 2359304 | tf_op jit(solution)/shard_map/ppermute | solution.py:635
  114.7 26.4 %collective-permute-start.7 = (bf16[1536,256]{1,0:T(8,128)(2,1)}, bf16[1536,256]{1,0:T(8,128)(2,1)S(1)}, u32[]{:S(2)}, u32[]{:S(2)}) collective-permute-start(bf16[1536,256]{1,0:T(8,128)(2,1)} %collective-permute-done.6.refs_10_.refs_12_.refs_11_), channel_id=1, source_target_pairs={{0,8},{4,12},{8,0},{12,4},{1,9},{5,13},{9,1},{13,5},{2,10},{6,14},... | collective-permute-start | bytes 2359304 | tf_op jit(solution)/shard_map/ppermute | solution.py:638
  117.2 40.0 %collective-permute-start.21 = (bf16[352,1024]{1,0:T(8,128)(2,1)}, bf16[352,1024]{1,0:T(8,128)(2,1)}, u32[]{:S(2)}, u32[]{:S(2)}) collective-permute-start(bf16[352,1024]{1,0:T(8,128)(2,1)} %dynamic-slice_bitcast_fusion), channel_id=1, source_target_pairs={{0,2},{1,3},{6,4},{7,5},{8,10},{9,11},{14,12},{15,13},{16,18},{17,... | collective-permute-start | bytes 2162696 | tf_op jit(solution)/shard_map/ppermute | solution.py:635
  124.5 16.6 %collective-permute-start.11 = (bf16[128,1024]{1,0:T(8,128)(2,1)S(1)}, bf16[128,1024]{1,0:T(8,128)(2,1)}, u32[]{:S(2)}, u32[]{:S(2)}) collective-permute-start(bf16[128,1024]{1,0:T(8,128)(2,1)S(1)} %collective-permute-done.10.refs_15_.refs_11_.refs_12_.refs_16_), channel_id=1, source_target_pairs={{0,8},{4,12},{8,0},{12,4},{1,9},{5,13},{9,1},{13,5},{2,10},{6,14},... | collective-permute-start | bytes 786440 | tf_op jit(solution)/shard_map/ppermute | solution.py:638
  150.1 13.1 %collective-permute-start.12 = (bf16[256,1024]{1,0:T(8,128)(2,1)}, bf16[256,1024]{1,0:T(8,128)(2,1)S(1)}, u32[]{:S(2)}, u32[]{:S(2)}) collective-permute-start(bf16[256,1024]{1,0:T(8,128)(2,1)} %get-tuple-element.72), channel_id=1, source_target_pairs={{0,4},{4,0},{8,12},{12,8},{1,5},{5,1},{9,13},{13,9},{2,6},{6,2},{1... | collective-permute-start | bytes 1572872 | tf_op jit(solution)/shard_map/ppermute | solution.py:638
  157.5 19.0 %collective-permute-start.23 = (bf16[352,1024]{1,0:T(8,128)(2,1)S(1)}, bf16[352,1024]{1,0:T(8,128)(2,1)}, u32[]{:S(2)}, u32[]{:S(2)}) collective-permute-start(bf16[352,1024]{1,0:T(8,128)(2,1)S(1)} %broadcast_select_fusion.18), channel_id=1, source_target_pairs={{0,16},{16,0},{1,17},{17,1},{2,18},{18,2},{3,19},{19,3},{4,20},{20... | collective-permute-start | bytes 2162696 | tf_op jit(solution)/shard_map/ppermute | solution.py:644
  159.1 66.7 %collective-permute-start.18 = (bf16[704,1024]{1,0:T(8,128)(2,1)}, bf16[704,1024]{1,0:T(8,128)(2,1)S(1)}, u32[]{:S(2)}, u32[]{:S(2)}) collective-permute-start(bf16[704,1024]{1,0:T(8,128)(2,1)} %broadcast_select_fusion.8), channel_id=1, source_target_pairs={{2,10},{3,11},{4,12},{5,13},{10,2},{11,3},{12,4},{13,5},{18,26},{1... | collective-permute-start | bytes 4325384 | tf_op jit(solution)/shard_map/ppermute | solution.py:635
  159.9 67.0 %collective-permute-start.20 = (bf16[704,1024]{1,0:T(8,128)(2,1)S(1)}, bf16[704,1024]{1,0:T(8,128)(2,1)}, u32[]{:S(2)}, u32[]{:S(2)}) collective-permute-start(bf16[704,1024]{1,0:T(8,128)(2,1)S(1)} %collective-permute-done.19.refs_8_.refs_10_), channel_id=1, source_target_pairs={{0,8},{4,12},{8,0},{12,4},{1,9},{5,13},{9,1},{13,5},{2,10},{6,14},... | collective-permute-start | bytes 4325384 | tf_op jit(solution)/shard_map/ppermute | solution.py:638
  161.5 21.2 %collective-permute-start.22 = (bf16[352,1024]{1,0:T(8,128)(2,1)S(1)}, bf16[352,1024]{1,0:T(8,128)(2,1)}, u32[]{:S(2)}, u32[]{:S(2)}) collective-permute-start(bf16[352,1024]{1,0:T(8,128)(2,1)S(1)} %broadcast_select_fusion.18), channel_id=1, source_target_pairs={{2,10},{3,11},{4,12},{5,13},{10,2},{11,3},{12,4},{13,5},{18,26},{1... | collective-permute-start | bytes 2162696 | tf_op jit(solution)/shard_map/ppermute | solution.py:635
  163.3 14.9 %collective-permute-start.13 = (bf16[128,1024]{1,0:T(8,128)(2,1)S(1)}, bf16[128,1024]{1,0:T(8,128)(2,1)S(1)}, u32[]{:S(2)}, u32[]{:S(2)}) collective-permute-start(bf16[128,1024]{1,0:T(8,128)(2,1)S(1)} %add_convert_fusion.19), channel_id=1, source_target_pairs={{0,1},{1,0},{2,3},{3,2},{4,5},{5,4},{6,7},{7,6},{8,9},{9,8},{10,11... | collective-permute-start | bytes 786440 | tf_op jit(solution)/shard_map/ppermute | solution.py:641
  176.5 49.2 %collective-permute-start.24 = (bf16[352,1024]{1,0:T(8,128)(2,1)}, bf16[352,1024]{1,0:T(8,128)(2,1)}, u32[]{:S(2)}, u32[]{:S(2)}) collective-permute-start(bf16[352,1024]{1,0:T(8,128)(2,1)} %collective-permute-done.23.refs_13_.refs_15_), channel_id=1, source_target_pairs={{0,8},{4,12},{8,0},{12,4},{1,9},{5,13},{9,1},{13,5},{2,10},{6,14},... | collective-permute-start | bytes 2162696 | tf_op jit(solution)/shard_map/ppermute | solution.py:638
  181.2 44.0 %collective-permute-start.14 = (bf16[128,1024]{1,0:T(8,128)(2,1)}, bf16[128,1024]{1,0:T(8,128)(2,1)S(1)}, u32[]{:S(2)}, u32[]{:S(2)}) collective-permute-start(bf16[128,1024]{1,0:T(8,128)(2,1)} %get-tuple-element.75.refs_1_.x0), channel_id=1, source_target_pairs={{0,1},{1,0},{2,3},{3,2},{4,5},{5,4},{6,7},{7,6},{8,9},{9,8},{10,11... | collective-permute-start | bytes 786440 | tf_op jit(solution)/shard_map/ppermute | solution.py:641
  182.7 43.9 %collective-permute-start.15 = (bf16[128,1024]{1,0:T(8,128)(2,1)}, bf16[128,1024]{1,0:T(8,128)(2,1)S(1)}, u32[]{:S(2)}, u32[]{:S(2)}) collective-permute-start(bf16[128,1024]{1,0:T(8,128)(2,1)} %get-tuple-element.75.refs_1_.x0), channel_id=1, source_target_pairs={{0,4},{4,0},{8,12},{12,8},{1,5},{5,1},{9,13},{13,9},{2,6},{6,2},{1... | collective-permute-start | bytes 786440 | tf_op jit(solution)/shard_map/ppermute | solution.py:638
  234.1 8.6 %collective-permute-start.25 = (bf16[256,1024]{1,0:T(8,128)(2,1)}, bf16[256,1024]{1,0:T(8,128)(2,1)S(1)}, u32[]{:S(2)}, u32[]{:S(2)}) collective-permute-start(bf16[256,1024]{1,0:T(8,128)(2,1)} %get-tuple-element.77), channel_id=1, source_target_pairs={{0,4},{4,0},{8,12},{12,8},{1,5},{5,1},{9,13},{13,9},{2,6},{6,2},{1... | collective-permute-start | bytes 1572872 | tf_op jit(solution)/shard_map/ppermute | solution.py:638
  243.9 8.7 %collective-permute-start.26 = (bf16[128,1024]{1,0:T(8,128)(2,1)S(1)}, bf16[128,1024]{1,0:T(8,128)(2,1)S(1)}, u32[]{:S(2)}, u32[]{:S(2)}) collective-permute-start(bf16[128,1024]{1,0:T(8,128)(2,1)S(1)} %add_convert_fusion.18), channel_id=1, source_target_pairs={{0,1},{1,0},{2,3},{3,2},{4,5},{5,4},{6,7},{7,6},{8,9},{9,8},{10,11... | collective-permute-start | bytes 786440 | tf_op jit(solution)/shard_map/ppermute | solution.py:641
  293.9 8.4 %collective-permute-start.33 = (bf16[128,1024]{1,0:T(8,128)(2,1)S(1)}, bf16[128,1024]{1,0:T(8,128)(2,1)S(1)}, u32[]{:S(2)}, u32[]{:S(2)}) collective-permute-start(bf16[128,1024]{1,0:T(8,128)(2,1)S(1)} %add_convert_fusion.17), channel_id=1, source_target_pairs={{0,1},{1,0},{2,3},{3,2},{4,5},{5,4},{6,7},{7,6},{8,9},{9,8},{10,11... | collective-permute-start | bytes 786440 | tf_op jit(solution)/shard_map/ppermute | solution.py:641
  305.3 9.5 %collective-permute-start.34 = (bf16[128,1024]{1,0:T(8,128)(2,1)}, bf16[128,1024]{1,0:T(8,128)(2,1)S(1)}, u32[]{:S(2)}, u32[]{:S(2)}) collective-permute-start(bf16[128,1024]{1,0:T(8,128)(2,1)} %get-tuple-element.88.refs_1_.x0), channel_id=1, source_target_pairs={{0,1},{1,0},{2,3},{3,2},{4,5},{5,4},{6,7},{7,6},{8,9},{9,8},{10,11... | collective-permute-start | bytes 786440 | tf_op jit(solution)/shard_map/ppermute | solution.py:641
  305.7 13.0 %collective-permute-start.40 = (bf16[128,1024]{1,0:T(8,128)(2,1)S(1)}, bf16[128,1024]{1,0:T(8,128)(2,1)S(1)}, u32[]{:S(2)}, u32[]{:S(2)}) collective-permute-start(bf16[128,1024]{1,0:T(8,128)(2,1)S(1)} %dynamic-slice_bitcast_fusion.1.refs_1_.residual.g0), channel_id=1, source_target_pairs={{0,1},{1,0},{2,3},{3,2},{4,5},{5,4},{6,7},{7,6},{8,9},{9,8},{10,11... | collective-permute-start | bytes 786440 | tf_op jit(solution)/shard_map/ppermute | solution.py:641
  307.5 11.2 %collective-permute-start.35 = (bf16[128,1024]{1,0:T(8,128)(2,1)}, bf16[128,1024]{1,0:T(8,128)(2,1)S(1)}, u32[]{:S(2)}, u32[]{:S(2)}) collective-permute-start(bf16[128,1024]{1,0:T(8,128)(2,1)} %get-tuple-element.88.refs_1_.x0), channel_id=1, source_target_pairs={{0,4},{4,0},{8,12},{12,8},{1,5},{5,1},{9,13},{13,9},{2,6},{6,2},{1... | collective-permute-start | bytes 786440 | tf_op jit(solution)/shard_map/ppermute | solution.py:638
  314.8 12.1 %collective-permute-start.41 = (bf16[128,1024]{1,0:T(8,128)(2,1)S(1)}, bf16[128,1024]{1,0:T(8,128)(2,1)S(1)}, u32[]{:S(2)}, u32[]{:S(2)}) collective-permute-start(bf16[128,1024]{1,0:T(8,128)(2,1)S(1)} %dynamic-slice_bitcast_fusion.1.refs_1_.residual.g0), channel_id=1, source_target_pairs={{0,4},{4,0},{8,12},{12,8},{1,5},{5,1},{9,13},{13,9},{2,6},{6,2},{1... | collective-permute-start | bytes 786440 | tf_op jit(solution)/shard_map/ppermute | solution.py:638
  338.0 8.7 %collective-permute-start.44 = (bf16[128,1024]{1,0:T(8,128)(2,1)S(1)}, bf16[128,1024]{1,0:T(8,128)(2,1)S(1)}, u32[]{:S(2)}, u32[]{:S(2)}) collective-permute-start(bf16[128,1024]{1,0:T(8,128)(2,1)S(1)} %add_convert_fusion.15), channel_id=1, source_target_pairs={{0,1},{1,0},{2,3},{3,2},{4,5},{5,4},{6,7},{7,6},{8,9},{9,8},{10,11... | collective-permute-start | bytes 786440 | tf_op jit(solution)/shard_map/ppermute | solution.py:641
  386.2 26.9 %collective-permute-start.37 = (bf16[256,1024]{1,0:T(8,128)(2,1)}, bf16[256,1024]{1,0:T(8,128)(2,1)S(1)}, u32[]{:S(2)}, u32[]{:S(2)}) collective-permute-start(bf16[256,1024]{1,0:T(8,128)(2,1)} %get-tuple-element.90), channel_id=1, source_target_pairs={{0,4},{4,0},{8,12},{12,8},{1,5},{5,1},{9,13},{13,9},{2,6},{6,2},{1... | collective-permute-start | bytes 1572872 | tf_op jit(solution)/shard_map/ppermute | solution.py:638
  395.6 57.4 %collective-permute-start.81 = (bf16[1056,1024]{1,0:T(8,128)(2,1)S(1)}, bf16[1056,1024]{1,0:T(8,128)(2,1)}, u32[]{:S(2)}, u32[]{:S(2)}) collective-permute-start(bf16[1056,1024]{1,0:T(8,128)(2,1)S(1)} %constant_dynamic-slice_fusion.3), channel_id=1, source_target_pairs={{0,8},{4,12},{8,0},{12,4},{1,9},{5,13},{9,1},{13,5},{2,10},{6,14},... | collective-permute-start | bytes 6488072 | tf_op jit(solution)/shard_map/ppermute | solution.py:638
  405.6 13.5 %collective-permute-start.53 = (bf16[128,1024]{1,0:T(8,128)(2,1)}, bf16[128,1024]{1,0:T(8,128)(2,1)S(1)}, u32[]{:S(2)}, u32[]{:S(2)}) collective-permute-start(bf16[128,1024]{1,0:T(8,128)(2,1)} %get-tuple-element.108.refs_1_.residual.g0), channel_id=1, source_target_pairs={{0,4},{4,0},{8,12},{12,8},{1,5},{5,1},{9,13},{13,9},{2,6},{6,2},{1... | collective-permute-start | bytes 786440 | tf_op jit(solution)/shard_map/ppermute | solution.py:638
  414.1 27.5 %collective-permute-start.38 = (bf16[128,1024]{1,0:T(8,128)(2,1)}, bf16[128,1024]{1,0:T(8,128)(2,1)S(1)}, u32[]{:S(2)}, u32[]{:S(2)}) collective-permute-start(bf16[128,1024]{1,0:T(8,128)(2,1)} %add_convert_fusion.16), channel_id=1, source_target_pairs={{0,1},{1,0},{2,3},{3,2},{4,5},{5,4},{6,7},{7,6},{8,9},{9,8},{10,11... | collective-permute-start | bytes 786440 | tf_op jit(solution)/shard_map/ppermute | solution.py:641
  426.8 13.3 %collective-permute-start.55 = (bf16[256,1024]{1,0:T(8,128)(2,1)}, bf16[256,1024]{1,0:T(8,128)(2,1)S(1)}, u32[]{:S(2)}, u32[]{:S(2)}) collective-permute-start(bf16[256,1024]{1,0:T(8,128)(2,1)} %get-tuple-element.112), channel_id=1, source_target_pairs={{0,4},{4,0},{8,12},{12,8},{1,5},{5,1},{9,13},{13,9},{2,6},{6,2},{1... | collective-permute-start | bytes 1572872 | tf_op jit(solution)/shard_map/ppermute | solution.py:638
  437.0 98.6 %collective-permute-start.75 = (bf16[1056,1024]{1,0:T(8,128)(2,1)}, bf16[1056,1024]{1,0:T(8,128)(2,1)}, u32[]{:S(2)}, u32[]{:S(2)}) collective-permute-start(bf16[1056,1024]{1,0:T(8,128)(2,1)} %constant_dynamic-slice_fusion), channel_id=1, source_target_pairs={{0,8},{4,12},{8,0},{12,4},{1,9},{5,13},{9,1},{13,5},{2,10},{6,14},... | collective-permute-start | bytes 6488072 | tf_op jit(solution)/shard_map/ppermute | solution.py:638
  438.9 74.7 %collective-permute-start.69 = (bf16[2048,256]{1,0:T(8,128)(2,1)}, bf16[2048,256]{1,0:T(8,128)(2,1)}, u32[]{:S(2)}, u32[]{:S(2)}) collective-permute-start(bf16[2048,256]{1,0:T(8,128)(2,1)} %constant_dynamic-slice_fusion.1), channel_id=1, source_target_pairs={{0,8},{4,12},{8,0},{12,4},{1,9},{5,13},{9,1},{13,5},{2,10},{6,14},... | collective-permute-start | bytes 3145736 | tf_op jit(solution)/shard_map/ppermute | solution.py:638
  451.6 8.9 %collective-permute-start.57 = (bf16[128,1024]{1,0:T(8,128)(2,1)}, bf16[128,1024]{1,0:T(8,128)(2,1)S(1)}, u32[]{:S(2)}, u32[]{:S(2)}) collective-permute-start(bf16[128,1024]{1,0:T(8,128)(2,1)} %get-tuple-element.114.refs_1_.g0), channel_id=1, source_target_pairs={{0,1},{1,0},{2,3},{3,2},{4,5},{5,4},{6,7},{7,6},{8,9},{9,8},{10,11... | collective-permute-start | bytes 786440 | tf_op jit(solution)/shard_map/ppermute | solution.py:641
  456.3 102.6 %collective-permute-start.82 = (bf16[1056,1024]{1,0:T(8,128)(2,1)S(1)}, bf16[1056,1024]{1,0:T(8,128)(2,1)}, u32[]{:S(2)}, u32[]{:S(2)}) collective-permute-start(bf16[1056,1024]{1,0:T(8,128)(2,1)S(1)} %add_convert_fusion.2), channel_id=1, source_target_pairs={{0,16},{1,17},{2,18},{3,19},{4,20},{5,21},{6,22},{7,23},{8,24},{9,... | collective-permute-start | bytes 6488072 | tf_op jit(solution)/shard_map/ppermute | solution.py:697
  460.4 58.4 %collective-permute-start.58 = (bf16[128,1024]{1,0:T(8,128)(2,1)S(1)}, bf16[128,1024]{1,0:T(8,128)(2,1)S(1)}, u32[]{:S(2)}, u32[]{:S(2)}) collective-permute-start(bf16[128,1024]{1,0:T(8,128)(2,1)S(1)} %copy-done.44), channel_id=1, source_target_pairs={{0,4},{4,0},{8,12},{12,8},{1,5},{5,1},{9,13},{13,9},{2,6},{6,2},{1... | collective-permute-start | bytes 786440 | tf_op jit(solution)/shard_map/ppermute | solution.py:638
  460.5 58.3 %collective-permute-start.59 = (bf16[128,1024]{1,0:T(8,128)(2,1)S(1)}, bf16[128,1024]{1,0:T(8,128)(2,1)S(1)}, u32[]{:S(2)}, u32[]{:S(2)}) collective-permute-start(bf16[128,1024]{1,0:T(8,128)(2,1)S(1)} %collective-permute-done.57.refs_2_.g1), channel_id=1, source_target_pairs={{0,4},{4,0},{8,12},{12,8},{1,5},{5,1},{9,13},{13,9},{2,6},{6,2},{1... | collective-permute-start | bytes 786440 | tf_op jit(solution)/shard_map/ppermute | solution.py:638
  515.3 27.9 %collective-permute-start.70 = (bf16[2048,256]{1,0:T(8,128)(2,1)S(1)}, bf16[2048,256]{1,0:T(8,128)(2,1)}, u32[]{:S(2)}, u32[]{:S(2)}) collective-permute-start(bf16[2048,256]{1,0:T(8,128)(2,1)S(1)} %add_convert_fusion.8), channel_id=1, source_target_pairs={{0,16},{1,17},{2,18},{3,19},{4,20},{5,21},{6,22},{7,23},{8,24},{9,... | collective-permute-start | bytes 3145736 | tf_op jit(solution)/shard_map/ppermute | solution.py:697
  534.4 24.1 %collective-permute-start.63 = (bf16[2048,256]{1,0:T(8,128)(2,1)S(1)}, bf16[2048,256]{1,0:T(8,128)(2,1)S(1)}, u32[]{:S(2)}, u32[]{:S(2)}) collective-permute-start(bf16[2048,256]{1,0:T(8,128)(2,1)S(1)} %constant_dynamic-slice_fusion.2), channel_id=1, source_target_pairs={{0,8},{4,12},{8,0},{12,4},{1,9},{5,13},{9,1},{13,5},{2,10},{6,14},... | collective-permute-start | bytes 3145736 | tf_op jit(solution)/shard_map/ppermute | solution.py:638
  538.2 52.0 %collective-permute-start.76 = (bf16[1056,1024]{1,0:T(8,128)(2,1)S(1)}, bf16[1056,1024]{1,0:T(8,128)(2,1)S(1)}, u32[]{:S(2)}, u32[]{:S(2)}) collective-permute-start(bf16[1056,1024]{1,0:T(8,128)(2,1)S(1)} %add_convert_fusion.5), channel_id=1, source_target_pairs={{16,0},{17,1},{18,2},{19,3},{20,4},{21,5},{22,6},{23,7},{24,8},{25... | collective-permute-start | bytes 6488072 | tf_op jit(solution)/shard_map/ppermute | solution.py:697
  540.4 153.6 %collective-permute-start.39 = (bf16[128,1024]{1,0:T(8,128)(2,1)}, bf16[128,1024]{1,0:T(8,128)(2,1)}, u32[]{:S(2)}, u32[]{:S(2)}) collective-permute-start(bf16[128,1024]{1,0:T(8,128)(2,1)} %broadcast_select_fusion.20), channel_id=1, source_target_pairs={{0,16},{16,0},{1,17},{17,1},{2,18},{18,2},{3,19},{19,3},{4,20},{20... | collective-permute-start | bytes 786440 | tf_op jit(solution)/shard_map/ppermute | solution.py:644
  544.7 73.8 %collective-permute-start.71 = (bf16[2048,256]{1,0:T(8,128)(2,1)S(1)}, bf16[2048,256]{1,0:T(8,128)(2,1)S(1)}, u32[]{:S(2)}, u32[]{:S(2)}) collective-permute-start(bf16[2048,256]{1,0:T(8,128)(2,1)S(1)} %add_convert_fusion.7), channel_id=1, source_target_pairs={{2,0},{3,1},{4,6},{5,7},{10,8},{11,9},{12,14},{13,15},{18,16},{19,... | collective-permute-start | bytes 3145736 | tf_op jit(solution)/shard_map/ppermute | solution.py:635
  558.9 57.1 %collective-permute-start.64 = (bf16[2048,256]{1,0:T(8,128)(2,1)S(1)}, bf16[2048,256]{1,0:T(8,128)(2,1)S(1)}, u32[]{:S(2)}, u32[]{:S(2)}) collective-permute-start(bf16[2048,256]{1,0:T(8,128)(2,1)S(1)} %add_convert_fusion.11), channel_id=1, source_target_pairs={{16,0},{17,1},{18,2},{19,3},{20,4},{21,5},{22,6},{23,7},{24,8},{25... | collective-permute-start | bytes 3145736 | tf_op jit(solution)/shard_map/ppermute | solution.py:697
  562.9 65.7 %collective-permute-start.83 = (bf16[1056,1024]{1,0:T(8,128)(2,1)S(1)}, bf16[1056,1024]{1,0:T(8,128)(2,1)S(1)}, u32[]{:S(2)}, u32[]{:S(2)}) collective-permute-start(bf16[1056,1024]{1,0:T(8,128)(2,1)S(1)} %add_convert_fusion.1), channel_id=1, source_target_pairs={{2,0},{3,1},{4,6},{5,7},{10,8},{11,9},{12,14},{13,15},{18,16},{19,... | collective-permute-start | bytes 6488072 | tf_op jit(solution)/shard_map/ppermute | solution.py:635
  590.2 30.9 %collective-permute-start.61 = (bf16[128,1024]{1,0:T(8,128)(2,1)S(1)}, bf16[128,1024]{1,0:T(8,128)(2,1)S(1)}, u32[]{:S(2)}, u32[]{:S(2)}) collective-permute-start(bf16[128,1024]{1,0:T(8,128)(2,1)S(1)} %add_convert_fusion.12), channel_id=1, source_target_pairs={{0,1},{1,0},{2,3},{3,2},{4,5},{5,4},{6,7},{7,6},{8,9},{9,8},{10,11... | collective-permute-start | bytes 786440 | tf_op jit(solution)/shard_map/ppermute | solution.py:641
  615.9 80.9 %collective-permute-start.77 = (bf16[1056,1024]{1,0:T(8,128)(2,1)S(1)}, bf16[1056,1024]{1,0:T(8,128)(2,1)}, u32[]{:S(2)}, u32[]{:S(2)}) collective-permute-start(bf16[1056,1024]{1,0:T(8,128)(2,1)S(1)} %add_convert_fusion.4), channel_id=1, source_target_pairs={{2,0},{3,1},{4,6},{5,7},{10,8},{11,9},{12,14},{13,15},{18,16},{19,... | collective-permute-start | bytes 6488072 | tf_op jit(solution)/shard_map/ppermute | solution.py:635
  618.5 72.7 %collective-permute-start.65 = (bf16[2048,256]{1,0:T(8,128)(2,1)}, bf16[2048,256]{1,0:T(8,128)(2,1)}, u32[]{:S(2)}, u32[]{:S(2)}) collective-permute-start(bf16[2048,256]{1,0:T(8,128)(2,1)} %add_convert_fusion.10), channel_id=1, source_target_pairs={{2,0},{3,1},{4,6},{5,7},{10,8},{11,9},{12,14},{13,15},{18,16},{19,... | collective-permute-start | bytes 3145736 | tf_op jit(solution)/shard_map/ppermute | solution.py:635
  621.1 169.1 %collective-permute-start.72 = (bf16[2048,256]{1,0:T(8,128)(2,1)}, bf16[2048,256]{1,0:T(8,128)(2,1)}, u32[]{:S(2)}, u32[]{:S(2)}) collective-permute-start(bf16[2048,256]{1,0:T(8,128)(2,1)} %add_convert_fusion.6), channel_id=1, source_target_pairs={{0,4},{1,5},{6,2},{7,3},{8,12},{9,13},{14,10},{15,11},{16,20},{17,... | collective-permute-start | bytes 3145736 | tf_op jit(solution)/shard_map/ppermute | solution.py:635
  630.0 76.9 %collective-permute-start.73 = (bf16[2048,256]{1,0:T(8,128)(2,1)}, bf16[2048,256]{1,0:T(8,128)(2,1)}, u32[]{:S(2)}, u32[]{:S(2)}) collective-permute-start(bf16[2048,256]{1,0:T(8,128)(2,1)} %add_convert_fusion.6), channel_id=1, source_target_pairs={{0,8},{1,9},{6,14},{7,15},{8,0},{9,1},{14,6},{15,7},{16,24},{17,25... | collective-permute-start | bytes 3145736 | tf_op jit(solution)/shard_map/ppermute | solution.py:635
  691.2 12.6 %collective-permute-start.62 = (bf16[128,1024]{1,0:T(8,128)(2,1)S(1)}, bf16[128,1024]{1,0:T(8,128)(2,1)}, u32[]{:S(2)}, u32[]{:S(2)}) collective-permute-start(bf16[128,1024]{1,0:T(8,128)(2,1)S(1)} %fusion.2), channel_id=1, source_target_pairs={{0,16},{16,0},{1,17},{17,1},{2,18},{18,2},{3,19},{19,3},{4,20},{20... | collective-permute-start | bytes 786440 | tf_op jit(solution)/shard_map/ppermute | solution.py:644
  694.0 103.3 %collective-permute-start.85 = (bf16[1056,1024]{1,0:T(8,128)(2,1)S(1)}, bf16[1056,1024]{1,0:T(8,128)(2,1)}, u32[]{:S(2)}, u32[]{:S(2)}) collective-permute-start(bf16[1056,1024]{1,0:T(8,128)(2,1)S(1)} %add_convert_fusion), channel_id=1, source_target_pairs={{0,8},{1,9},{6,14},{7,15},{8,0},{9,1},{14,6},{15,7},{16,24},{17,25... | collective-permute-start | bytes 6488072 | tf_op jit(solution)/shard_map/ppermute | solution.py:635
  696.9 94.7 %collective-permute-start.67 = (bf16[2048,256]{1,0:T(8,128)(2,1)}, bf16[2048,256]{1,0:T(8,128)(2,1)}, u32[]{:S(2)}, u32[]{:S(2)}) collective-permute-start(bf16[2048,256]{1,0:T(8,128)(2,1)} %add_convert_fusion.9), channel_id=1, source_target_pairs={{0,8},{1,9},{6,14},{7,15},{8,0},{9,1},{14,6},{15,7},{16,24},{17,25... | collective-permute-start | bytes 3145736 | tf_op jit(solution)/shard_map/ppermute | solution.py:635
  703.8 101.8 %collective-permute-start.79 = (bf16[1056,1024]{1,0:T(8,128)(2,1)}, bf16[1056,1024]{1,0:T(8,128)(2,1)}, u32[]{:S(2)}, u32[]{:S(2)}) collective-permute-start(bf16[1056,1024]{1,0:T(8,128)(2,1)} %add_convert_fusion.3), channel_id=1, source_target_pairs={{0,8},{1,9},{6,14},{7,15},{8,0},{9,1},{14,6},{15,7},{16,24},{17,25... | collective-permute-start | bytes 6488072 | tf_op jit(solution)/shard_map/ppermute | solution.py:635
  706.9 87.7 %collective-permute-start.74 = (bf16[2048,256]{1,0:T(8,128)(2,1)}, bf16[2048,256]{1,0:T(8,128)(2,1)}, u32[]{:S(2)}, u32[]{:S(2)}) collective-permute-start(bf16[2048,256]{1,0:T(8,128)(2,1)} %collective-permute-done.73), channel_id=1, source_target_pairs={{0,4},{1,5},{6,2},{7,3},{8,12},{9,13},{14,10},{15,11},{16,20},{17,... | collective-permute-start | bytes 3145736 | tf_op jit(solution)/shard_map/ppermute | solution.py:635
  790.2 12.6 %collective-permute-start.66 = (bf16[2048,256]{1,0:T(8,128)(2,1)}, bf16[2048,256]{1,0:T(8,128)(2,1)S(1)}, u32[]{:S(2)}, u32[]{:S(2)}) collective-permute-start(bf16[2048,256]{1,0:T(8,128)(2,1)} %add_convert_fusion.9), channel_id=1, source_target_pairs={{0,4},{1,5},{6,2},{7,3},{8,12},{9,13},{14,10},{15,11},{16,20},{17,... | collective-permute-start | bytes 3145736 | tf_op jit(solution)/shard_map/ppermute | solution.py:635
  791.6 16.6 %collective-permute-start.68 = (bf16[2048,256]{1,0:T(8,128)(2,1)}, bf16[2048,256]{1,0:T(8,128)(2,1)S(1)}, u32[]{:S(2)}, u32[]{:S(2)}) collective-permute-start(bf16[2048,256]{1,0:T(8,128)(2,1)} %collective-permute-done.67), channel_id=1, source_target_pairs={{0,4},{1,5},{6,2},{7,3},{8,12},{9,13},{14,10},{15,11},{16,20},{17,... | collective-permute-start | bytes 3145736 | tf_op jit(solution)/shard_map/ppermute | solution.py:635
  794.6 21.3 %collective-permute-start.84 = (bf16[1056,1024]{1,0:T(8,128)(2,1)S(1)}, bf16[1056,1024]{1,0:T(8,128)(2,1)}, u32[]{:S(2)}, u32[]{:S(2)}) collective-permute-start(bf16[1056,1024]{1,0:T(8,128)(2,1)S(1)} %add_convert_fusion), channel_id=1, source_target_pairs={{0,4},{1,5},{6,2},{7,3},{8,12},{9,13},{14,10},{15,11},{16,20},{17,... | collective-permute-start | bytes 6488072 | tf_op jit(solution)/shard_map/ppermute | solution.py:635
  797.3 18.6 %collective-permute-start.86 = (bf16[1056,1024]{1,0:T(8,128)(2,1)}, bf16[1056,1024]{1,0:T(8,128)(2,1)}, u32[]{:S(2)}, u32[]{:S(2)}) collective-permute-start(bf16[1056,1024]{1,0:T(8,128)(2,1)} %collective-permute-done.85), channel_id=1, source_target_pairs={{0,4},{1,5},{6,2},{7,3},{8,12},{9,13},{14,10},{15,11},{16,20},{17,... | collective-permute-start | bytes 6488072 | tf_op jit(solution)/shard_map/ppermute | solution.py:635
  802.8 15.2 %collective-permute-start.78 = (bf16[1056,1024]{1,0:T(8,128)(2,1)}, bf16[1056,1024]{1,0:T(8,128)(2,1)}, u32[]{:S(2)}, u32[]{:S(2)}) collective-permute-start(bf16[1056,1024]{1,0:T(8,128)(2,1)} %add_convert_fusion.3), channel_id=1, source_target_pairs={{0,4},{1,5},{6,2},{7,3},{8,12},{9,13},{14,10},{15,11},{16,20},{17,... | collective-permute-start | bytes 6488072 | tf_op jit(solution)/shard_map/ppermute | solution.py:635
  805.6 12.4 %collective-permute-start.80 = (bf16[1056,1024]{1,0:T(8,128)(2,1)}, bf16[1056,1024]{1,0:T(8,128)(2,1)}, u32[]{:S(2)}, u32[]{:S(2)}) collective-permute-start(bf16[1056,1024]{1,0:T(8,128)(2,1)} %collective-permute-done.79), channel_id=1, source_target_pairs={{0,4},{1,5},{6,2},{7,3},{8,12},{9,13},{14,10},{15,11},{16,20},{17,... | collective-permute-start | bytes 6488072 | tf_op jit(solution)/shard_map/ppermute | solution.py:635
  (108 other events, 1479.7 us)
